TPU v7x, 32 devices: a whole 2x2x4 slice. The times are simulated.
32 devices in a mesh: wide: 16 (over z, x, core), narrow: 2 (over y).
Axes of the slice: x: 2, y: 2, z: 4, core: 2. Of those that a mesh axis runs over, the one named last changes fastest.
Arguments:
- patch_input: bfloat16 [32, 2048, 768], P('wide', 'narrow'), may hold values from -6 to 6
- text_input: bfloat16 [32, 1024, 768], P('wide', 'narrow'), may hold values from -6 to 6
- patch_cotangent: bfloat16 [32, 2048, 768], P('wide', 'narrow'), may hold values from -6 to 6
- text_cotangent: bfloat16 [32, 1024, 768], P('wide', 'narrow'), may hold values from -6 to 6
- patch_count: int32 [32], P('wide'), may hold values from 1024 to 2048, as said below
- header_len: int32 [32], P('wide'), may hold values from 128 to 512, as said below
- text_len: int32 [32], P('wide'), may hold values from 256 to 1024, as said below
- norm_gains: bfloat16 [768, 6], P('wide'), may hold values from 0.25 to 1.75
- header_embed: bfloat16 [768], P('wide'), may hold values from -3 to 3
- enc_project: bfloat16 [768, 2304], P('wide'), may hold values from -0.21875 to 0.21875
- enc_output: bfloat16 [768, 768], P('wide'), may hold values from -6 to 6
- enc_gate_up: bfloat16 [768, 4096], P('wide'), may hold values from -0.21875 to 0.21875
- enc_down: bfloat16 [2048, 768], P('wide'), may hold values from -0.25 to 0.25
- self_project: bfloat16 [768, 2304], P('wide'), may hold values from -0.21875 to 0.21875
- self_output: bfloat16 [768, 768], P('wide'), may hold values from -1.5 to 1.5
- cross_project: bfloat16 [768, 2304], P('wide'), may hold values from -0.21875 to 0.21875
- cross_output: bfloat16 [768, 768], P('wide'), may hold values from -6 to 6
- dec_gate_up: bfloat16 [768, 4096], P('wide'), may hold values from -0.21875 to 0.21875
- dec_down: bfloat16 [2048, 768], P('wide'), may hold values from -0.25 to 0.25
Outputs:
- patch_output: bfloat16 [32, 2048, 768], P('wide', 'narrow')
- text_output: bfloat16 [32, 1024, 768], P('wide', 'narrow')
- patch_input_grad: float32 [32, 2048, 768], P('wide', 'narrow')
- text_input_grad: float32 [32, 1024, 768], P('wide', 'narrow')
- norm_gains_grad: float32 [768, 6], P('wide')
- header_embed_grad: float32 [768], P('wide')
- enc_project_grad: float32 [768, 2304], P('wide')
- enc_output_grad: float32 [768, 768], P('wide')
- enc_gate_up_grad: float32 [768, 4096], P('wide')
- enc_down_grad: float32 [2048, 768], P('wide')
- self_project_grad: float32 [768, 2304], P('wide')
- self_output_grad: float32 [768, 768], P('wide')
- cross_project_grad: float32 [768, 2304], P('wide')
- cross_output_grad: float32 [768, 768], P('wide')
- dec_gate_up_grad: float32 [768, 4096], P('wide')
- dec_down_grad: float32 [2048, 768], P('wide')
Inputs may be any that keep to these rules, and one draw needn't show every extreme that they name: `patch_count`: in each aligned group of 2 items, one item has all 2048 patches; rows at or past an item's count are padding. `header_len`: less than the item's patch_count. `text_len`: in each aligned group of 2 items, one item has all 1024 tokens.
All inputs are finite; a program needn't handle non-finite values.
Results may differ from a plain program's by a relative error of at most 0.022.
Values may be sent and summed in bfloat16 or wider, within the bound.
No kernel may reach another device: no remote copies, remote signals or barrier semaphores. Data moves between devices by JAX's collectives and lax.ppermute only.
A program may use at most 280 MiB of HBM per device.

v0:
```python
import math

import jax
import jax.numpy as jnp
from jax import lax
from jax.sharding import PartitionSpec as P

D = 768
HEADS = 12
HEAD_DIM = 64
FF = 2048


EPSILON = 1e-06
NEGATIVE = -1e30


def rms_norm(values, gain_row):
    inverse = lax.rsqrt(jnp.mean(values * values, axis=-1, keepdims=True) + EPSILON)
    normed = values * inverse
    return (normed * gain_row, normed, inverse)


def rms_back(gradient, normed, inverse, gain_row):
    gain_grad = jnp.sum(gradient * normed, axis=0)
    scaled = gradient * gain_row
    inner_mean = jnp.mean(scaled * normed, axis=-1, keepdims=True)
    return (inverse * (scaled - normed * inner_mean), gain_grad)


def matmul(left_side, right_side):
    return jnp.dot(left_side, right_side, preferred_element_type=jnp.float32)


def matmul_back(left_side, right_side):
    return lax.dot_general(
        left_side, right_side, (((1,), (1,)), ((), ())), preferred_element_type=jnp.float32
    )


def gated_gelu(gate_values):
    return jax.nn.gelu(gate_values[:, :FF], approximate=True) * gate_values[:, FF:]


def fetch_weights(first_array, second_array, third_array):
    return (
        lax.all_gather(first_array, "wide", axis=0, tiled=True),
        lax.all_gather(second_array, "wide", axis=0, tiled=True),
        lax.all_gather(third_array, "wide", axis=0, tiled=True),
    )


def reduce_rows(term_rows, shard_rows):
    return lax.psum_scatter(
        term_rows(jnp.int32(0), lax.axis_size("wide") * shard_rows).astype(jnp.bfloat16),
        "wide",
        scatter_dimension=0,
        tiled=True,
    ).astype(jnp.float32)


def weight_grad(left_side, right_side):
    shard_rows = left_side.shape[1] // lax.axis_size("wide")

    def term_rows(first_row, row_span):
        return lax.dot_general(
            left_side, right_side, (((0,), (0,)), ((), ())), preferred_element_type=jnp.float32
        )

    return reduce_rows(term_rows, shard_rows)


def vector_grad(full_term):
    shard_rows = full_term.shape[0] // lax.axis_size("wide")

    def term_rows(first_row, row_span):
        return full_term

    return reduce_rows(term_rows, shard_rows)


def block_scores(head_queries, key_block, first_key, query_pos, key_limit, causal):
    block_width = key_block.shape[0]
    key_pos = first_key + jnp.arange(block_width, dtype=jnp.int32)
    scores = jnp.einsum(
        "qhd,khd->hqk", head_queries, key_block, preferred_element_type=jnp.float32
    ) * HEAD_DIM ** (-0.5)
    allowed = jnp.broadcast_to(key_pos[None, :] < key_limit, (query_pos.shape[0], block_width))
    if causal:
        allowed = jnp.logical_and(allowed, key_pos[None, :] <= query_pos[:, None])
    return (jnp.where(allowed[None], scores, NEGATIVE), allowed[None])


def split_keys(key_all, value_all):
    key_total = key_all.shape[0]
    block_width = math.gcd(key_total, 256)
    steps_count = key_total // block_width
    head_keys = key_all.reshape(steps_count, block_width, HEADS, HEAD_DIM)
    head_values = value_all.reshape(steps_count, block_width, HEADS, HEAD_DIM)
    first_keys = jnp.arange(steps_count, dtype=jnp.int32) * block_width
    return (head_keys, head_values, first_keys)


def attend_forward(queries, key_local, value_local, key_limit, causal):
    key_all, value_all = (
        lax.all_gather(key_local, "narrow", axis=0, tiled=True),
        lax.all_gather(value_local, "narrow", axis=0, tiled=True),
    )
    query_count = queries.shape[0]
    head_queries = queries.reshape(query_count, HEADS, HEAD_DIM)
    query_pos = lax.axis_index("narrow") * query_count + jnp.arange(query_count, dtype=jnp.int32)
    head_keys, head_values, first_keys = split_keys(key_all, value_all)

    def statistics(running, inputs):
        running_max, running_sum = running
        key_block, first_key = inputs
        masked, allowed = block_scores(
            head_queries, key_block, first_key, query_pos, key_limit, causal
        )
        new_max = jnp.maximum(running_max, jnp.max(masked, axis=-1))
        weights = jnp.where(allowed, jnp.exp(masked - new_max[..., None]), 0.0)
        new_sum = running_sum * jnp.exp(running_max - new_max) + jnp.sum(weights, axis=-1)
        return ((new_max, new_sum), None)

    start_max = jnp.full((HEADS, query_count), NEGATIVE, jnp.float32)
    start_sum = jnp.zeros((HEADS, query_count), jnp.float32)
    (row_max, row_sum), unused = lax.scan(
        statistics, (start_max, start_sum), (head_keys, first_keys)
    )
    log_total = row_max + jnp.log(row_sum)

    def outputs(summed, inputs):
        key_block, value_block, first_key = inputs
        masked, allowed = block_scores(
            head_queries, key_block, first_key, query_pos, key_limit, causal
        )
        weights = jnp.where(allowed, jnp.exp(masked - log_total[..., None]), 0.0).astype(
            jnp.bfloat16
        )
        return (
            summed
            + jnp.einsum("hqk,khd->qhd", weights, value_block, preferred_element_type=jnp.float32),
            None,
        )

    start_rows = jnp.zeros((query_count, HEADS, HEAD_DIM), jnp.float32)
    attended, unused = lax.scan(outputs, start_rows, (head_keys, head_values, first_keys))
    return (attended.reshape(query_count, D), log_total, key_all, value_all)


def attend_backward(queries, key_all, value_all, log_total, head_grad_in, key_limit, causal):
    query_count = queries.shape[0]
    head_queries = queries.reshape(query_count, HEADS, HEAD_DIM)
    head_grad = head_grad_in.reshape(query_count, HEADS, HEAD_DIM)
    query_pos = lax.axis_index("narrow") * query_count + jnp.arange(query_count, dtype=jnp.int32)
    head_keys, head_values, first_keys = split_keys(key_all, value_all)

    def recompute(key_block, value_block, first_key):
        masked, allowed = block_scores(
            head_queries, key_block, first_key, query_pos, key_limit, causal
        )
        weights = jnp.where(allowed, jnp.exp(masked - log_total[..., None]), 0.0)
        prob_grad = jnp.einsum(
            "qhd,khd->hqk", head_grad, value_block, preferred_element_type=jnp.float32
        )
        return (weights, prob_grad)

    def weighted(summed, inputs):
        key_block, value_block, first_key = inputs
        weights, prob_grad = recompute(key_block, value_block, first_key)
        return (summed + jnp.sum(weights * prob_grad, axis=-1), None)

    weighted_sum, unused = lax.scan(
        weighted, jnp.zeros((HEADS, query_count), jnp.float32), (head_keys, head_values, first_keys)
    )

    def gradients(summed, inputs):
        key_block, value_block, first_key = inputs
        weights, prob_grad = recompute(key_block, value_block, first_key)
        score_grad = (weights * (prob_grad - weighted_sum[..., None]) * HEAD_DIM ** (-0.5)).astype(
            jnp.bfloat16
        )
        summed = summed + jnp.einsum(
            "hqk,khd->qhd", score_grad, key_block, preferred_element_type=jnp.float32
        )
        key_grad = jnp.einsum(
            "hqk,qhd->khd", score_grad, head_queries, preferred_element_type=jnp.float32
        )
        value_grad = jnp.einsum(
            "hqk,qhd->khd",
            weights.astype(jnp.bfloat16),
            head_grad,
            preferred_element_type=jnp.float32,
        )
        return (summed, (key_grad, value_grad))

    start_rows = jnp.zeros((query_count, HEADS, HEAD_DIM), jnp.float32)
    query_grad, (key_grads, value_grads) = lax.scan(
        gradients, start_rows, (head_keys, head_values, first_keys)
    )
    key_total = key_all.shape[0]
    key_own, value_own = (
        lax.psum_scatter(
            key_grads.reshape(key_total, D).astype(jnp.bfloat16),
            "narrow",
            scatter_dimension=0,
            tiled=True,
        ).astype(jnp.float32),
        lax.psum_scatter(
            value_grads.reshape(key_total, D).astype(jnp.bfloat16),
            "narrow",
            scatter_dimension=0,
            tiled=True,
        ).astype(jnp.float32),
    )
    return (
        query_grad.reshape(query_count, D).astype(jnp.bfloat16),
        key_own.astype(jnp.bfloat16),
        value_own.astype(jnp.bfloat16),
    )


def encoder_forward(patch_input, header_mask, patch_count, first_group, second_group):
    item_count = patch_input.shape[0]
    patch_rows = patch_input.shape[1]
    gain_full = first_group[0].astype(jnp.float32)
    header_full = first_group[1].astype(jnp.float32)
    start_rows = patch_input.astype(jnp.float32) + header_mask[:, :, None] * header_full
    start_flat = start_rows.reshape(item_count * patch_rows, D)
    attn_normed, attn_unit, attn_inverse = rms_norm(start_flat, gain_full[:, 0])
    attn_input = attn_normed.astype(jnp.bfloat16)
    projected = (
        matmul(attn_input, first_group[2])
        .astype(jnp.bfloat16)
        .reshape(item_count, patch_rows, 3 * D)
    )
    attended_parts = []
    kept_keys = []
    for item_index in range(item_count):
        attended, log_total, key_all, value_all = attend_forward(
            projected[item_index, :, :D],
            projected[item_index, :, D : 2 * D],
            projected[item_index, :, 2 * D :],
            patch_count[item_index],
            False,
        )
        attended_parts.append(attended)
        kept_keys.append((log_total, key_all, value_all))
    attended_all = jnp.concatenate(attended_parts, axis=0).astype(jnp.bfloat16)
    middle = start_flat + matmul(attended_all, second_group[0])
    mlp_normed, mlp_unit, mlp_inverse = rms_norm(middle, gain_full[:, 1])
    mlp_input = mlp_normed.astype(jnp.bfloat16)
    gate_values = matmul(mlp_input, second_group[1])
    hidden = gated_gelu(gate_values).astype(jnp.bfloat16)
    output_rows = middle + matmul(hidden, second_group[2])
    return (
        attn_unit,
        attn_inverse,
        attn_input,
        projected,
        kept_keys,
        attended_all,
        mlp_unit,
        mlp_inverse,
        mlp_input,
        gate_values,
        hidden,
        output_rows,
    )


def on_device(
    patch_input,
    text_input,
    patch_cotangent,
    text_cotangent,
    patch_count,
    header_len,
    text_len,
    norm_gains,
    header_embed,
    enc_project,
    enc_output,
    enc_gate_up,
    enc_down,
    self_project,
    self_output,
    cross_project,
    cross_output,
    dec_gate_up,
    dec_down,
):
    item_count = patch_input.shape[0]
    patch_rows = patch_input.shape[1]
    text_rows = text_input.shape[1]
    patch_pos = lax.axis_index("narrow") * patch_rows + jnp.arange(patch_rows, dtype=jnp.int32)
    header_mask = (patch_pos[None, :] < header_len[:, None]).astype(jnp.float32)
    first_group = fetch_weights(norm_gains, header_embed, enc_project)
    second_group = fetch_weights(enc_output, enc_gate_up, enc_down)
    encoder_state = encoder_forward(
        patch_input, header_mask, patch_count, first_group, second_group
    )
    patch_final = encoder_state[11]
    third_group = fetch_weights(self_project, self_output, cross_project)
    fourth_group = fetch_weights(cross_output, dec_gate_up, dec_down)
    gain_full = first_group[0].astype(jnp.float32)
    text_flat = text_input.astype(jnp.float32).reshape(item_count * text_rows, D)
    self_normed, self_unit, self_inverse = rms_norm(text_flat, gain_full[:, 2])
    self_input = self_normed.astype(jnp.bfloat16)
    self_qkv = (
        matmul(self_input, third_group[0])
        .astype(jnp.bfloat16)
        .reshape(item_count, text_rows, 3 * D)
    )
    self_parts = []
    self_kept = []
    for item_index in range(item_count):
        attended, log_total, key_all, value_all = attend_forward(
            self_qkv[item_index, :, :D],
            self_qkv[item_index, :, D : 2 * D],
            self_qkv[item_index, :, 2 * D :],
            text_len[item_index],
            True,
        )
        self_parts.append(attended)
        self_kept.append((log_total, key_all, value_all))
    self_attended = jnp.concatenate(self_parts, axis=0).astype(jnp.bfloat16)
    text_middle = text_flat + matmul(self_attended, third_group[1])
    cross_normed, cross_unit, cross_inverse = rms_norm(text_middle, gain_full[:, 3])
    cross_input = cross_normed.astype(jnp.bfloat16)
    memory_normed, memory_unit, memory_inverse = rms_norm(patch_final, gain_full[:, 4])
    memory_input = memory_normed.astype(jnp.bfloat16)
    cross_queries = (
        matmul(cross_input, third_group[2][:, :D])
        .astype(jnp.bfloat16)
        .reshape(item_count, text_rows, D)
    )
    memory_kv = (
        matmul(memory_input, third_group[2][:, D:])
        .astype(jnp.bfloat16)
        .reshape(item_count, patch_rows, 2 * D)
    )
    cross_parts = []
    cross_kept = []
    for item_index in range(item_count):
        attended, log_total, key_all, value_all = attend_forward(
            cross_queries[item_index],
            memory_kv[item_index, :, :D],
            memory_kv[item_index, :, D:],
            patch_count[item_index],
            False,
        )
        cross_parts.append(attended)
        cross_kept.append((log_total, key_all, value_all))
    cross_attended = jnp.concatenate(cross_parts, axis=0).astype(jnp.bfloat16)
    text_late = text_middle + matmul(cross_attended, fourth_group[0])
    ffn_normed, ffn_unit, ffn_inverse = rms_norm(text_late, gain_full[:, 5])
    ffn_input = ffn_normed.astype(jnp.bfloat16)
    ffn_gate_values = matmul(ffn_input, fourth_group[1])
    ffn_hidden = gated_gelu(ffn_gate_values).astype(jnp.bfloat16)
    text_final = text_late + matmul(ffn_hidden, fourth_group[2])
    first_group = fetch_weights(norm_gains, header_embed, enc_project)
    fourth_group = fetch_weights(cross_output, dec_gate_up, dec_down)
    third_group = fetch_weights(self_project, self_output, cross_project)
    gain_full = first_group[0].astype(jnp.float32)
    text_grad = text_cotangent.astype(jnp.float32).reshape(item_count * text_rows, D)
    ffn_out_grad = text_grad.astype(jnp.bfloat16)
    grad_dec_down = weight_grad(ffn_hidden, ffn_out_grad)
    ffn_hidden_grad = matmul_back(ffn_out_grad, fourth_group[2])
    ffn_gate_grad = jax.vjp(gated_gelu, ffn_gate_values)[1](ffn_hidden_grad)[0].astype(jnp.bfloat16)
    grad_dec_gate_up = weight_grad(ffn_input, ffn_gate_grad)
    ffn_in_grad, gain_ffn = rms_back(
        matmul_back(ffn_gate_grad, fourth_group[1]), ffn_unit, ffn_inverse, gain_full[:, 5]
    )
    late_grad = text_grad + ffn_in_grad
    cross_out_grad = late_grad.astype(jnp.bfloat16)
    grad_cross_output = weight_grad(cross_attended, cross_out_grad)
    cross_head_grad = (
        matmul_back(cross_out_grad, fourth_group[0])
        .astype(jnp.bfloat16)
        .reshape(item_count, text_rows, D)
    )
    query_parts = []
    memory_parts = []
    for item_index in range(item_count):
        log_total, key_all, value_all = cross_kept[item_index]
        query_grad, key_grad, value_grad = attend_backward(
            cross_queries[item_index],
            key_all,
            value_all,
            log_total,
            cross_head_grad[item_index],
            patch_count[item_index],
            False,
        )
        query_parts.append(query_grad)
        memory_parts.append(jnp.concatenate([key_grad, value_grad], axis=1))
    cross_query_grad = jnp.concatenate(query_parts, axis=0)
    memory_kv_grad = jnp.concatenate(memory_parts, axis=0)

    def cross_rows(first_row, row_span):
        query_part = lax.dot_general(
            cross_input,
            cross_query_grad,
            (((0,), (0,)), ((), ())),
            preferred_element_type=jnp.float32,
        )
        memory_part = lax.dot_general(
            memory_input,
            memory_kv_grad,
            (((0,), (0,)), ((), ())),
            preferred_element_type=jnp.float32,
        )
        return jnp.concatenate([query_part, memory_part], axis=1)

    grad_cross_project = reduce_rows(cross_rows, D // lax.axis_size("wide"))
    query_in_grad, gain_cross = rms_back(
        matmul_back(cross_query_grad, third_group[2][:, :D]),
        cross_unit,
        cross_inverse,
        gain_full[:, 3],
    )
    memory_grad, gain_memory = rms_back(
        matmul_back(memory_kv_grad, third_group[2][:, D:]),
        memory_unit,
        memory_inverse,
        gain_full[:, 4],
    )
    middle_grad = late_grad + query_in_grad
    self_out_grad = middle_grad.astype(jnp.bfloat16)
    grad_self_output = weight_grad(self_attended, self_out_grad)
    self_head_grad = (
        matmul_back(self_out_grad, third_group[1])
        .astype(jnp.bfloat16)
        .reshape(item_count, text_rows, D)
    )
    self_grad_parts = []
    for item_index in range(item_count):
        log_total, key_all, value_all = self_kept[item_index]
        query_grad, key_grad, value_grad = attend_backward(
            self_qkv[item_index, :, :D],
            key_all,
            value_all,
            log_total,
            self_head_grad[item_index],
            text_len[item_index],
            True,
        )
        self_grad_parts.append(jnp.concatenate([query_grad, key_grad, value_grad], axis=1))
    self_qkv_grad = jnp.concatenate(self_grad_parts, axis=0)
    grad_self_project = weight_grad(self_input, self_qkv_grad)
    self_in_grad, gain_self = rms_back(
        matmul_back(self_qkv_grad, third_group[0]), self_unit, self_inverse, gain_full[:, 2]
    )
    text_input_grad = (middle_grad + self_in_grad).reshape(item_count, text_rows, D)
    second_group = fetch_weights(enc_output, enc_gate_up, enc_down)
    (
        attn_unit,
        attn_inverse,
        attn_input,
        projected,
        kept_keys,
        enc_attended,
        mlp_unit,
        mlp_inverse,
        mlp_input,
        enc_gate_values,
        enc_hidden,
        patch_again,
    ) = encoder_forward(patch_input, header_mask, patch_count, first_group, second_group)
    patch_grad = (
        patch_cotangent.astype(jnp.float32).reshape(item_count * patch_rows, D) + memory_grad
    )
    down_grad = patch_grad.astype(jnp.bfloat16)
    grad_enc_down = weight_grad(enc_hidden, down_grad)
    enc_hidden_grad = matmul_back(down_grad, second_group[2])
    enc_gate_grad = jax.vjp(gated_gelu, enc_gate_values)[1](enc_hidden_grad)[0].astype(jnp.bfloat16)
    grad_enc_gate_up = weight_grad(mlp_input, enc_gate_grad)
    mlp_in_grad, gain_mlp = rms_back(
        matmul_back(enc_gate_grad, second_group[1]), mlp_unit, mlp_inverse, gain_full[:, 1]
    )
    enc_middle_grad = patch_grad + mlp_in_grad
    enc_out_grad = enc_middle_grad.astype(jnp.bfloat16)
    grad_enc_output = weight_grad(enc_attended, enc_out_grad)
    enc_head_grad = (
        matmul_back(enc_out_grad, second_group[0])
        .astype(jnp.bfloat16)
        .reshape(item_count, patch_rows, D)
    )
    enc_grad_parts = []
    for item_index in range(item_count):
        log_total, key_all, value_all = kept_keys[item_index]
        query_grad, key_grad, value_grad = attend_backward(
            projected[item_index, :, :D],
            key_all,
            value_all,
            log_total,
            enc_head_grad[item_index],
            patch_count[item_index],
            False,
        )
        enc_grad_parts.append(jnp.concatenate([query_grad, key_grad, value_grad], axis=1))
    enc_qkv_grad = jnp.concatenate(enc_grad_parts, axis=0)
    grad_enc_project = weight_grad(attn_input, enc_qkv_grad)
    attn_in_grad, gain_attn = rms_back(
        matmul_back(enc_qkv_grad, first_group[2]), attn_unit, attn_inverse, gain_full[:, 0]
    )
    start_grad = enc_middle_grad + attn_in_grad
    header_flat = header_mask.reshape(item_count * patch_rows)
    header_term = jnp.sum(start_grad * header_flat[:, None], axis=0)
    gain_term = jnp.stack(
        [gain_attn, gain_mlp, gain_self, gain_cross, gain_memory, gain_ffn], axis=1
    )
    grad_gains = vector_grad(gain_term)
    grad_header = vector_grad(header_term)
    summed = (
        lax.psum(grad_gains.astype(jnp.bfloat16), "narrow").astype(jnp.float32),
        lax.psum(grad_header.astype(jnp.bfloat16), "narrow").astype(jnp.float32),
        lax.psum(grad_enc_project.astype(jnp.bfloat16), "narrow").astype(jnp.float32),
        lax.psum(grad_enc_output.astype(jnp.bfloat16), "narrow").astype(jnp.float32),
        lax.psum(grad_enc_gate_up.astype(jnp.bfloat16), "narrow").astype(jnp.float32),
        lax.psum(grad_enc_down.astype(jnp.bfloat16), "narrow").astype(jnp.float32),
        lax.psum(grad_self_project.astype(jnp.bfloat16), "narrow").astype(jnp.float32),
        lax.psum(grad_self_output.astype(jnp.bfloat16), "narrow").astype(jnp.float32),
        lax.psum(grad_cross_project.astype(jnp.bfloat16), "narrow").astype(jnp.float32),
        lax.psum(grad_cross_output.astype(jnp.bfloat16), "narrow").astype(jnp.float32),
        lax.psum(grad_dec_gate_up.astype(jnp.bfloat16), "narrow").astype(jnp.float32),
        lax.psum(grad_dec_down.astype(jnp.bfloat16), "narrow").astype(jnp.float32),
    )
    patch_output = patch_final.astype(jnp.bfloat16).reshape(item_count, patch_rows, D)
    text_output = text_final.astype(jnp.bfloat16).reshape(item_count, text_rows, D)
    patch_input_grad = start_grad.reshape(item_count, patch_rows, D)
    return (
        patch_output,
        text_output,
        patch_input_grad,
        text_input_grad,
        summed[0],
        summed[1],
        summed[2],
        summed[3],
        summed[4],
        summed[5],
        summed[6],
        summed[7],
        summed[8],
        summed[9],
        summed[10],
        summed[11],
    )


def solution(mesh):
    placed = (
        P("wide", "narrow", None),
        P("wide", "narrow", None),
        P("wide", "narrow", None),
        P("wide", "narrow", None),
        P("wide"),
        P("wide"),
        P("wide"),
        P("wide", None),
        P("wide"),
        P("wide", None),
        P("wide", None),
        P("wide", None),
        P("wide", None),
        P("wide", None),
        P("wide", None),
        P("wide", None),
        P("wide", None),
        P("wide", None),
        P("wide", None),
    )
    return jax.shard_map(
        on_device,
        mesh=mesh,
        in_specs=placed,
        out_specs=(
            P("wide", "narrow", None),
            P("wide", "narrow", None),
            P("wide", "narrow", None),
            P("wide", "narrow", None),
            P("wide", None),
            P("wide"),
            P("wide", None),
            P("wide", None),
            P("wide", None),
            P("wide", None),
            P("wide", None),
            P("wide", None),
            P("wide", None),
            P("wide", None),
            P("wide", None),
            P("wide", None),
        ),
        check_vma=False,
    )
```

profile of v0, /device:TPU:0, one launch (start us, length us, event | category | flops | bytes accessed | tf_op | source)
XLA Modules:
  0.0 3701.2 jit_solution(16206271239159204594)
XLA Ops:
  159.8 135.3 %while.318 = (s32[]{:T(128)}, f32[12,1024]{1,0:T(8,128)S(1)}, f32[12,1024]{1,0:T(8,128)S(1)}, s32[8]{0:T(128)S(1)}, s32[]{:T(128)}, /*index=5*/bf16[8,256,12,64]...) while((s32[]{:T(128)}, f32[12,1024]{1,0:T(8,128)S(1)}, ...), condition=%wide.region_4.5_spmd.clone, body=%wide.region_1.4_spmd.clone.sunk | while | flops 427880960 | bytes 27772284 | solution.py:127
  300.6 80.8 %while.319 = (s32[]{:T(128)}, f32[1024,12,64]{0,2,1:T(8,128)}, bf16[8,256,12,64]{1,3,2,0:T(8,128)(2,1)}, s32[8]{0:T(128)S(1)}, s32[]{:T(128)}, /*index=5*/bf16[8...) while((s32[]{:T(128)}, f32[1024,12,64]{0,2,1:T(8,128)}, ...), condition=%wide.region_6.7_spmd.clone, body=%wide.region_5.6_spmd.clone.sunk | while | flops 822608384 | bytes 8701571 | solution.py:147
  390.7 134.2 %while.320 = (s32[]{:T(128)}, f32[12,1024]{1,0:T(8,128)S(1)}, f32[12,1024]{1,0:T(8,128)S(1)}, s32[8]{0:T(128)S(1)}, s32[]{:T(128)}, /*index=5*/bf16[8,256,12,64]...) while((s32[]{:T(128)}, f32[12,1024]{1,0:T(8,128)S(1)}, ...), condition=%wide.region_10.11_spmd.clone, body=%wide.region_7.10_spmd.clone.sunk | while | flops 427880960 | bytes 27772284 | solution.py:127
  530.3 80.2 %while.321 = (s32[]{:T(128)}, f32[1024,12,64]{0,2,1:T(8,128)}, bf16[8,256,12,64]{1,3,2,0:T(8,128)(2,1)}, s32[8]{0:T(128)S(1)}, s32[]{:T(128)}, /*index=5*/bf16[8...) while((s32[]{:T(128)}, f32[1024,12,64]{0,2,1:T(8,128)}, ...), condition=%wide.region_12.13_spmd.clone, body=%wide.region_11.12_spmd.clone.sunk | while | flops 822608384 | bytes 8701571 | solution.py:147
  703.4 46.6 %while.322 = (s32[]{:T(128)}, f32[12,512]{1,0:T(8,128)S(1)}, f32[12,512]{1,0:T(8,128)}, s32[4]{0:T(128)S(1)}, s32[]{:T(128)}, /*index=5*/bf16[4,256,12,64]{1,3,2...) while((s32[]{:T(128)}, f32[12,512]{1,0:T(8,128)S(1)}, ...), condition=%wide.region_18.19_spmd.clone, body=%wide.region_15.18_spmd.clone.sunk | while | flops 214203648 | bytes 14678728 | solution.py:127
  796.8 44.3 %while.324 = (s32[]{:T(128)}, f32[12,512]{1,0:T(8,128)S(1)}, f32[12,512]{1,0:T(8,128)S(1)}, s32[4]{0:T(128)S(1)}, s32[]{:T(128)}, /*index=5*/bf16[4,256,12,64]{1...) while((s32[]{:T(128)}, f32[12,512]{1,0:T(8,128)S(1)}, ...), condition=%wide.region_24.25_spmd.clone, body=%wide.region_21.24_spmd.clone.sunk | while | flops 214203648 | bytes 14482064 | solution.py:127
  894.8 93.7 %while.326 = (s32[]{:T(128)}, f32[12,512]{1,0:T(8,128)S(1)}, f32[12,512]{1,0:T(8,128)S(1)}, s32[8]{0:T(128)S(1)}, s32[]{:T(128)}, /*index=5*/bf16[8,256,12,64]{1...) while((s32[]{:T(128)}, f32[12,512]{1,0:T(8,128)S(1)}, ...), condition=%wide.region_32.33_spmd.clone, body=%wide.region_29.32_spmd.clone.sunk | while | flops 213940736 | bytes 14083452 | solution.py:127
  993.9 45.4 %while.327 = (s32[]{:T(128)}, f32[512,12,64]{0,2,1:T(8,128)S(1)}, bf16[8,256,12,64]{1,3,2,0:T(8,128)(2,1)}, s32[8]{0:T(128)S(1)}, s32[]{:T(128)}, /*index=5*/bf1...) while((s32[]{:T(128)}, f32[512,12,64]{0,2,1:T(8,128)S(1)}, ...), condition=%wide.region_34.35_spmd.clone, body=%wide.region_33.34_spmd.clone.sunk | while | flops 411304448 | bytes 4744835 | solution.py:147
  1045.7 92.4 %while.328 = (s32[]{:T(128)}, f32[12,512]{1,0:T(8,128)S(1)}, f32[12,512]{1,0:T(8,128)S(1)}, s32[8]{0:T(128)S(1)}, s32[]{:T(128)}, /*index=5*/bf16[8,256,12,64]{1...) while((s32[]{:T(128)}, f32[12,512]{1,0:T(8,128)S(1)}, ...), condition=%wide.region_38.39_spmd.clone, body=%wide.region_35.38_spmd.clone.sunk | while | flops 213940736 | bytes 14083452 | solution.py:127
  1143.6 44.5 %while.329 = (s32[]{:T(128)}, f32[512,12,64]{0,2,1:T(8,128)S(1)}, bf16[8,256,12,64]{1,3,2,0:T(8,128)(2,1)}, s32[8]{0:T(128)S(1)}, s32[]{:T(128)}, /*index=5*/bf1...) while((s32[]{:T(128)}, f32[512,12,64]{0,2,1:T(8,128)S(1)}, ...), condition=%wide.region_40.41_spmd.clone, body=%wide.region_39.40_spmd.clone.sunk | while | flops 411304448 | bytes 4744835 | solution.py:147
  1248.5 59.6 %while.330 = (s32[]{:T(128)}, f32[12,512]{1,0:T(8,128)S(1)}, s32[8]{0:T(128)S(1)}, s32[]{:T(128)}, bf16[8,256,12,64]{1,3,2,0:T(8,128)(2,1)}, /*index=5*/bf16[512...) while((s32[]{:T(128)}, f32[12,512]{1,0:T(8,128)S(1)}, ...), condition=%wide.region_45.46_spmd.clone, body=%wide.region_43.45_spmd.clone.sunk | while | flops 412097024 | bytes 15066763 | solution.py:173
  1313.1 150.5 %while.331 = (s32[]{:T(128)}, f32[512,12,64]{0,2,1:T(8,128)S(1)}, bf16[8,256,12,64]{1,3,2,0:T(8,128)(2,1)}, bf16[8,256,12,64]{1,3,2,0:T(8,128)(2,1)}, bf16[8,256...) while((s32[]{:T(128)}, f32[512,12,64]{0,2,1:T(8,128)S(1)}, ...), condition=%wide.region_47.48_spmd.clone, body=%wide.region_46.47_spmd.clone.sunk | while | flops 1027867136 | bytes 103493136 | solution.py:198
  1477.7 59.3 %while.332 = (s32[]{:T(128)}, f32[12,512]{1,0:T(8,128)S(1)}, s32[8]{0:T(128)S(1)}, s32[]{:T(128)}, bf16[8,256,12,64]{1,3,2,0:T(8,128)(2,1)}, /*index=5*/bf16[512...) while((s32[]{:T(128)}, f32[12,512]{1,0:T(8,128)S(1)}, ...), condition=%wide.region_52.53_spmd.clone, body=%wide.region_50.52_spmd.clone.sunk | while | flops 412097024 | bytes 15066763 | solution.py:173
  1541.2 141.2 %while.333 = (s32[]{:T(128)}, f32[512,12,64]{0,2,1:T(8,128)S(1)}, bf16[8,256,12,64]{1,3,2,0:T(8,128)(2,1)}, bf16[8,256,12,64]{1,3,2,0:T(8,128)(2,1)}, bf16[8,256...) while((s32[]{:T(128)}, f32[512,12,64]{0,2,1:T(8,128)S(1)}, ...), condition=%wide.region_54.55_spmd.clone, body=%wide.region_53.54_spmd.clone.sunk | while | flops 1027867136 | bytes 100347376 | solution.py:198
  1704.5 32.0 while.338
  1740.3 80.3 %while.339 = (s32[]{:T(128)}, f32[512,12,64]{0,2,1:T(8,128)S(1)}, bf16[4,256,12,64]{1,3,2,0:T(8,128)(2,1)}, bf16[4,256,12,64]{1,3,2,0:T(8,128)(2,1)}, bf16[4,256...) while((s32[]{:T(128)}, f32[512,12,64]{0,2,1:T(8,128)S(1)}, ...), condition=%wide.region_79.80_spmd.clone, body=%wide.region_78.79_spmd.clone.sunk | while | flops 1028130048 | bytes 107038008 | solution.py:198
  1864.1 77.3 %while.341 = (s32[]{:T(128)}, f32[512,12,64]{0,2,1:T(8,128)S(1)}, bf16[4,256,12,64]{1,3,2,0:T(8,128)(2,1)}, bf16[4,256,12,64]{1,3,2,0:T(8,128)(2,1)}, bf16[4,256...) while((s32[]{:T(128)}, f32[512,12,64]{0,2,1:T(8,128)S(1)}, ...), condition=%wide.region_86.87_spmd.clone, body=%wide.region_85.86_spmd.clone.sunk | while | flops 1028130048 | bytes 100746504 | solution.py:198
  1974.8 33.6 fusion.380
  2043.8 85.4 %while.334 = (s32[]{:T(128)}, f32[12,1024]{1,0:T(8,128)S(1)}, s32[8]{0:T(128)S(1)}, s32[]{:T(128)}, bf16[8,256,12,64]{1,3,2,0:T(8,128)(2,1)}, /*index=5*/bf16[10...) while((s32[]{:T(128)}, f32[12,1024]{1,0:T(8,128)S(1)}, ...), condition=%wide.region_61.62_spmd.clone, body=%wide.region_59.61_spmd.clone.sunk | while | flops 824193536 | bytes 35636900 | solution.py:173
  2133.3 259.2 %while.335 = (s32[]{:T(128)}, f32[1024,12,64]{0,2,1:T(8,128)}, bf16[8,256,12,64]{1,3,2,0:T(8,128)(2,1)}, bf16[8,256,12,64]{1,3,2,0:T(8,128)(2,1)}, bf16[8,256,12...) while((s32[]{:T(128)}, f32[1024,12,64]{0,2,1:T(8,128)}, ...), condition=%wide.region_63.64_spmd.clone, body=%wide.region_62.63_spmd.clone.sunk | while | flops 2055733760 | bytes 147607008 | solution.py:198
  2400.6 84.1 %while.336 = (s32[]{:T(128)}, f32[12,1024]{1,0:T(8,128)S(1)}, s32[8]{0:T(128)S(1)}, s32[]{:T(128)}, bf16[8,256,12,64]{1,3,2,0:T(8,128)(2,1)}, /*index=5*/bf16[10...) while((s32[]{:T(128)}, f32[12,1024]{1,0:T(8,128)S(1)}, ...), condition=%wide.region_68.69_spmd.clone, body=%wide.region_66.68_spmd.clone.sunk | while | flops 824193536 | bytes 29345416 | solution.py:173
  2495.5 258.0 %while.337 = (s32[]{:T(128)}, f32[1024,12,64]{0,2,1:T(8,128)}, bf16[8,256,12,64]{1,3,2,0:T(8,128)(2,1)}, bf16[8,256,12,64]{1,3,2,0:T(8,128)(2,1)}, bf16[8,256,12...) while((s32[]{:T(128)}, f32[1024,12,64]{0,2,1:T(8,128)}, ...), condition=%wide.region_70.71_spmd.clone, body=%wide.region_69.70_spmd.clone.sunk | while | flops 2055733760 | bytes 147607008 | solution.py:198
  2919.9 44.0 %multiply_reduce_fusion.7 = (bf16[768]{0:T(1024)(128)(2,1)S(1)}, f32[2048]{0:T(1024)S(1)}, f32[2048,768]{1,0:T(8,128)}) fusion(f32[2,1024,768]{2,1,0:T(8,128)} %copy-done.27, f32[2048]{0:T(1024)S(1)} %bitcast.1169, f32[768]{0:T(1024)S(1)} %copy-done.105, bf16[768,2304]{1,0:T(8,128)(2,1)S(1)} %copy-done.144, bf16[1024,768]{0,1:T(8,128)(2,1)S(1)} %copy-done.148, ...), kind=kOutput, calls=%fused_computation.460 | convolution fusion | flops 7313814528 | bytes 25580032 | tf_op jit(solution)/shard_map/dot_general | solution.py:36
  2972.5 68.9 %reduce-scatter.68.cloned.1.call-done = bf16[128,768]{1,0:T(8,128)(2,1)} async-done(((bf16[2048,768]{1,0:T(8,128)(2,1)}), bf16[128,768]{1,0:T(8,128)(2,1)}) %reduce-scatter.68.cloned.1.call-update) | async-done | bytes 196624 | tf_op jit(solution)/shard_map/reduce_scatter | solution.py:54
  3041.4 60.5 %reduce-scatter.52.cloned.1.call-done = bf16[48,768]{1,0:T(8,128)(2,1)} async-done(((bf16[768,768]{1,0:T(8,128)(2,1)}), bf16[48,768]{1,0:T(8,128)(2,1)}) %reduce-scatter.52.cloned.1.call-update) | async-done | bytes 73744 | tf_op jit(solution)/shard_map/reduce_scatter | solution.py:54
  3102.0 70.8 %reduce-scatter.58.cloned.1.call-done = bf16[48,2304]{1,0:T(8,128)(2,1)} async-done(((bf16[768,2304]{1,0:T(8,128)(2,1)}), bf16[48,2304]{1,0:T(8,128)(2,1)}) %reduce-scatter.58.cloned.1.call-update) | async-done | bytes 221200 | tf_op jit(solution)/shard_map/reduce_scatter | solution.py:54
  3172.7 88.1 %reduce-scatter.66.cloned.1.call-done = bf16[48,4096]{1,0:T(8,128)(2,1)} async-done(((bf16[768,4096]{1,0:T(8,128)(2,1)}), bf16[48,4096]{1,0:T(8,128)(2,1)}) %reduce-scatter.66.cloned.1.call-update) | async-done | bytes 393232 | tf_op jit(solution)/shard_map/reduce_scatter | solution.py:54
  3260.9 69.7 %reduce-scatter.56.cloned.1.call-done = bf16[128,768]{1,0:T(8,128)(2,1)} async-done(((bf16[2048,768]{1,0:T(8,128)(2,1)}), bf16[128,768]{1,0:T(8,128)(2,1)}) %reduce-scatter.56.cloned.1.call-update) | async-done | bytes 196624 | tf_op jit(solution)/shard_map/reduce_scatter | solution.py:54
  3330.5 71.4 %reduce-scatter.62.cloned.1.call-done = bf16[48,2304]{1,0:T(8,128)(2,1)} async-done(((bf16[768,2304]{1,0:T(8,128)(2,1)}), bf16[48,2304]{1,0:T(8,128)(2,1)}) %reduce-scatter.62.cloned.1.call-update) | async-done | bytes 221200 | tf_op jit(solution)/shard_map/reduce_scatter | solution.py:54
  3401.9 88.4 %reduce-scatter.54.cloned.1.call-done = bf16[48,4096]{1,0:T(8,128)(2,1)} async-done(((bf16[768,4096]{1,0:T(8,128)(2,1)}), bf16[48,4096]{1,0:T(8,128)(2,1)}) %reduce-scatter.54.cloned.1.call-update) | async-done | bytes 393232 | tf_op jit(solution)/shard_map/reduce_scatter | solution.py:54
  3490.3 71.2 %reduce-scatter.50.cloned.1.call-done = bf16[48,2304]{1,0:T(8,128)(2,1)} async-done(((bf16[768,2304]{1,0:T(8,128)(2,1)}), bf16[48,2304]{1,0:T(8,128)(2,1)}) %reduce-scatter.50.cloned.1.call-update) | async-done | bytes 221200 | tf_op jit(solution)/shard_map/reduce_scatter | solution.py:54
  3624.7 58.8 %all-reduce.10.cloned.1.call-done = (bf16[48,2304]{1,0:T(8,128)(2,1)}, bf16[48,768]{1,0:T(8,128)(2,1)}, bf16[48,4096]{1,0:T(8,128)(2,1)}, bf16[128,768]{1,0:T(8,...) async-done(((bf16[48,2304]{1,0:T(8,128)(2,1)}, ...) | async-done | bytes 2064400 | tf_op jit(solution)/shard_map/psum | solution.py:519
  (1886 shorter events, 3040.1 us)
Async XLA Ops:
  94.4 430.5 %all-gather.60.cloned.1.call-start = ((), (), s32[]{:S(2)}) async-start(), calls=%async_computation.57 | async-start | bytes 4718592 | tf_op jit(solution)/shard_map/all_gather | solution.py:107
  96.2 518.3 %all-gather.38.cloned.1.call-start = ((), (), s32[]{:S(2)}) async-start(), calls=%async_computation.24 | async-start | bytes 1253376 | tf_op jit(solution)/shard_map/all_gather | solution.py:47
  96.9 526.8 %all-gather.40.cloned.1.call-start = ((), (), s32[]{:S(2)}) async-start(), calls=%async_computation.25 | async-start | bytes 6684672 | tf_op jit(solution)/shard_map/all_gather | solution.py:48
  97.7 564.5 %all-gather.42.cloned.1.call-start = ((), (), s32[]{:S(2)}) async-start(), calls=%async_computation.26 | async-start | bytes 3342336 | tf_op jit(solution)/shard_map/all_gather | solution.py:49
  98.4 576.7 %all-gather.48.cloned.1.call-start = ((), (), s32[]{:S(2)}) async-start(), calls=%async_computation.29 | async-start | bytes 3760128 | tf_op jit(solution)/shard_map/all_gather | solution.py:49
  99.0 598.4 %all-gather.66.cloned.1.call-start = ((), (), s32[]{:S(2)}) async-start(), calls=%async_computation.60 | async-start | bytes 2359296 | tf_op jit(solution)/shard_map/all_gather | solution.py:106
  117.6 632.4 %all-gather.64.cloned.1.call-start = ((), (), s32[]{:S(2)}) async-start(), calls=%async_computation.59 | async-start | bytes 2359296 | tf_op jit(solution)/shard_map/all_gather | solution.py:107
  118.9 672.2 %all-gather.70.cloned.1.call-start = ((), (), s32[]{:S(2)}) async-start(), calls=%async_computation.62 | async-start | bytes 2359296 | tf_op jit(solution)/shard_map/all_gather | solution.py:106
  120.2 720.9 %all-gather.68.cloned.1.call-start = ((), (), s32[]{:S(2)}) async-start(), calls=%async_computation.61 | async-start | bytes 2359296 | tf_op jit(solution)/shard_map/all_gather | solution.py:107
  121.4 760.2 %all-gather.46.cloned.1.call-start = ((), (), s32[]{:S(2)}) async-start(), calls=%async_computation.28 | async-start | bytes 1253376 | tf_op jit(solution)/shard_map/all_gather | solution.py:48
  122.0 767.4 %all-gather.74.cloned.1.call-start = ((), (), s32[]{:S(2)}) async-start(), calls=%async_computation.64 | async-start | bytes 4718592 | tf_op jit(solution)/shard_map/all_gather | solution.py:106
  692.2 445.9 %all-gather.76.cloned.1.call-start = ((), (), s32[]{:S(2)}) async-start(), calls=%async_computation.65 | async-start | bytes 4718592 | tf_op jit(solution)/shard_map/all_gather | solution.py:107
  693.9 495.3 %all-gather.50.cloned.1.call-start = ((), (), s32[]{:S(2)}) async-start(), calls=%async_computation.30 | async-start | bytes 1253376 | tf_op jit(solution)/shard_map/all_gather | solution.py:47
  694.5 500.7 %all-gather.52.cloned.1.call-start = ((), (), s32[]{:S(2)}) async-start(), calls=%async_computation.31 | async-start | bytes 6684672 | tf_op jit(solution)/shard_map/all_gather | solution.py:48
  695.2 513.1 %all-gather.54.cloned.1.call-start = ((), (), s32[]{:S(2)}) async-start(), calls=%async_computation.32 | async-start | bytes 3342336 | tf_op jit(solution)/shard_map/all_gather | solution.py:49
  696.0 1254.6 %reduce-scatter.26.cloned.1.call-start = ((), (), s32[]{:S(2)}) async-start(), calls=%async_computation.33 | async-start | bytes 4718592 | tf_op jit(solution)/shard_map/reduce_scatter | solution.py:203
  1470.9 479.7 %reduce-scatter.28.cloned.1.call-start = ((), (), s32[]{:S(2)}) async-start(), calls=%async_computation.34 | async-start | bytes 4718592 | tf_op jit(solution)/shard_map/reduce_scatter | solution.py:209
  1537.0 413.7 %reduce-scatter.30.cloned.1.call-start = ((), (), s32[]{:S(2)}) async-start(), calls=%async_computation.35 | async-start | bytes 4718592 | tf_op jit(solution)/shard_map/reduce_scatter | solution.py:203
  1737.5 1057.3 %reduce-scatter.42.cloned.1.call-start = ((), (), s32[]{:S(2)}) async-start(), calls=%async_computation.41 | async-start | bytes 2359296 | tf_op jit(solution)/shard_map/reduce_scatter | solution.py:203
  1825.3 969.6 %reduce-scatter.44.cloned.1.call-start = ((), (), s32[]{:S(2)}) async-start(), calls=%async_computation.42 | async-start | bytes 2359296 | tf_op jit(solution)/shard_map/reduce_scatter | solution.py:209
  1861.4 933.5 %reduce-scatter.46.cloned.1.call-start = ((), (), s32[]{:S(2)}) async-start(), calls=%async_computation.43 | async-start | bytes 2359296 | tf_op jit(solution)/shard_map/reduce_scatter | solution.py:203
  1946.1 848.8 %reduce-scatter.48.cloned.1.call-start = ((), (), s32[]{:S(2)}) async-start(), calls=%async_computation.44 | async-start | bytes 2359296 | tf_op jit(solution)/shard_map/reduce_scatter | solution.py:209
  1950.4 934.9 %reduce-scatter.34.cloned.1.call-start = ((), (), s32[]{:S(2)}) async-start(), calls=%async_computation.37 | async-start | bytes 4718592 | tf_op jit(solution)/shard_map/reduce_scatter | solution.py:203
  2399.2 486.2 %reduce-scatter.36.cloned.1.call-start = ((), (), s32[]{:S(2)}) async-start(), calls=%async_computation.38 | async-start | bytes 4718592 | tf_op jit(solution)/shard_map/reduce_scatter | solution.py:209
  2491.3 394.0 %reduce-scatter.38.cloned.1.call-start = ((), (), s32[]{:S(2)}) async-start(), calls=%async_computation.39 | async-start | bytes 4718592 | tf_op jit(solution)/shard_map/reduce_scatter | solution.py:203
  2806.4 454.4 %reduce-scatter.66.cloned.1.call-start = ((), (), s32[]{:S(2)}) async-start(), calls=%async_computation.53 | async-start | bytes 6684672 | tf_op jit(solution)/shard_map/reduce_scatter | solution.py:54
  2824.6 506.0 %reduce-scatter.56.cloned.1.call-start = ((), (), s32[]{:S(2)}) async-start(), calls=%async_computation.48 | async-start | bytes 3342336 | tf_op jit(solution)/shard_map/reduce_scatter | solution.py:54
  2837.2 564.7 %reduce-scatter.62.cloned.1.call-start = ((), (), s32[]{:S(2)}) async-start(), calls=%async_computation.51 | async-start | bytes 3760128 | tf_op jit(solution)/shard_map/reduce_scatter | solution.py:54
  2856.7 633.7 %reduce-scatter.54.cloned.1.call-start = ((), (), s32[]{:S(2)}) async-start(), calls=%async_computation.47 | async-start | bytes 6684672 | tf_op jit(solution)/shard_map/reduce_scatter | solution.py:54
  2880.3 681.2 %reduce-scatter.50.cloned.1.call-start = ((), (), s32[]{:S(2)}) async-start(), calls=%async_computation.45 | async-start | bytes 3760128 | tf_op jit(solution)/shard_map/reduce_scatter | solution.py:54
  2903.0 714.8 %reduce-scatter.70.cloned.1.call-start = ((), (), s32[]{:S(2)}) async-start(), calls=%async_computation.67 | async-start | bytes 208896
  2964.9 718.7 %all-reduce.10.cloned.1.call-start = ((), (), s32[]{:S(2)}) async-start(), calls=%async_computation.68 | async-start | bytes 4128768 | tf_op jit(solution)/shard_map/psum | solution.py:519
  (288 other events, 4756.8 us)
Sparse Core Ops, SparseCore 0:
  10.3 50.0 all-gather.35
  62.7 46.2 all-gather.43
  110.5 43.9 all-gather.57
  155.9 44.9 all-gather.55
  202.3 44.9 all-gather.61
  248.6 44.9 all-gather.59
  336.5 60.7 all-gather.39
  399.7 44.0 all-gather.41
  445.8 46.0 all-gather.47
  688.0 45.1 all-gather.73
  734.5 44.9 all-gather.71
  780.9 44.9 all-gather.77
  828.0 44.9 all-gather.75
  915.8 60.6 all-gather.51
  978.7 44.0 all-gather.53
  1471.1 43.6 reduce-scatter.25
  1537.2 43.6 reduce-scatter.27
  1703.7 43.6 reduce-scatter.29
  2399.3 43.6 reduce-scatter.33
  2760.3 43.6 reduce-scatter.37
  2853.9 58.0 reduce-scatter.63
  2915.5 56.9 reduce-scatter.59
  2976.2 65.2 reduce-scatter.67
  3045.0 56.8 reduce-scatter.51
  3105.7 66.9 reduce-scatter.57
  3176.7 84.1 reduce-scatter.65
  3265.1 65.3 reduce-scatter.55
  3334.9 66.9 reduce-scatter.61
  3406.2 84.0 reduce-scatter.53
  3494.2 67.2 reduce-scatter.49
  3565.4 52.4 reduce-scatter.69
  3620.6 62.8 all-reduce.9
  (14 shorter events, 457.6 us)
where the time goes:
time: 3720 us; the launch traced here: 3700 us
  matrix products  1910 us (51%)
  waiting for transfers between devices  707 us (19%)
  other arithmetic  538 us (14%)
  local copies, waits for them, and re-layouts  428 us (12%)
  blocking collectives  88.4 us (2%)
    reduce_scatter x10, waiting for transfers between devices, reduce_rows(): lax.psum_scatter(term_rows(jnp.int32(0), lax.axis_size('wide') * shard_ro...  596 us
    dot_general x120, matrix products, block_scores(): jnp.einsum('qhd,khd->hqk', head_queries, key_block, preferred_element_typ...  431 us
    dot_general x80, matrix products, recompute(): jnp.einsum('qhd,khd->hqk', head_grad, value_block, preferred_element_type...  408 us
    dot_general x40, matrix products, outputs(): jnp.einsum('hqk,khd->qhd', weights, value_block, preferred_element_type=j...  229 us
    reduce_sum x40, other arithmetic, statistics(): jnp.sum(weights, axis=-1)  217 us
    lt x160, other arithmetic, block_scores(): key_pos[None, :] < key_limit  203 us
    dot_general x40, matrix products, gradients(): jnp.einsum('hqk,khd->qhd', score_grad, key_block, preferred_element_type=...  177 us
    dot_general x40, matrix products, gradients(): jnp.einsum('hqk,qhd->khd', weights.astype(jnp.bfloat16), head_grad, prefe...  176 us
  transfers between devices with their start and end apart: 46, of which 13 were waited for; matrix products, arithmetic and copies ran while one was open for 67% of the time, Pallas kernels for 0%

commit v1 on v0

v1 whole, which is shorter than its diff:
```python
import functools
import math

import jax
import jax.numpy as jnp
from jax import lax
from jax.experimental import pallas as pl
from jax.experimental.pallas import tpu as pltpu
from jax.sharding import PartitionSpec as P

D = 768
HEADS = 12
HEAD_DIM = 64
FF = 2048
PAIR = 2 * HEAD_DIM
PAIRS = HEADS // 2
FF_BLOCK = 256
GELU_SCALE = 0.7978845608028654
GELU_CUBE = 0.044715


EPSILON = 1e-06
NEGATIVE = -1e30
BF16 = jnp.bfloat16
F32 = jnp.float32


def rms_scale(values):
    return lax.rsqrt(jnp.mean(values * values, axis=-1, keepdims=True) + EPSILON)


def rms_norm(values, gain_row):
    inverse = rms_scale(values)
    return (values * inverse * gain_row).astype(BF16)


def matmul(left_side, right_side):
    return jnp.dot(left_side, right_side, preferred_element_type=F32)


def matmul_back(left_side, right_side):
    return lax.dot_general(
        left_side, right_side, (((1,), (1,)), ((), ())), preferred_element_type=F32
    )


def dot(left_side, right_side):
    return jnp.dot(left_side, right_side, preferred_element_type=F32)


def lanes_of(rows):
    return lax.broadcasted_iota(jnp.int32, (rows, PAIR), 1)


def place(lane, first_lane, columns):
    filled = jnp.zeros(lane.shape, F32)
    for offset, column in enumerate(columns):
        filled = jnp.where(lane == first_lane + offset, column, filled)
    return filled


def three_parts(values):
    high = values.astype(BF16).astype(F32)
    rest = values - high
    middle = rest.astype(BF16).astype(F32)
    return (high, middle, (rest - middle).astype(BF16).astype(F32))


def both_heads(lane, pair_values, columns):
    first = jnp.where(lane < HEAD_DIM, pair_values, place(lane, HEAD_DIM, columns))
    second = jnp.where(lane >= HEAD_DIM, pair_values, place(lane, 0, columns))
    return (first.astype(BF16), second.astype(BF16))


def key_bias(first_key, rows, limit):
    position = first_key + lax.broadcasted_iota(jnp.int32, (rows, PAIR), 0)
    return jnp.where(position < limit, 0.0, NEGATIVE)


def forward_kernel(
    causal,
    aligned,
    scalars_ref,
    query_ref,
    key_ref,
    value_ref,
    out_ref,
    exact_ref,
    total_ref,
    key_first,
    key_second,
    value_first,
    value_second,
    key_bound,
):
    item = pl.program_id(0)
    block = pl.program_id(2)
    block_rows = query_ref.shape[1]
    key_total = key_ref.shape[1]
    limit = scalars_ref[1 + item]
    query_start = scalars_ref[0]

    def longest(lane, pair_values):
        square = pair_values * pair_values
        first = jnp.sum(jnp.where(lane < HEAD_DIM, square, 0.0), axis=1, keepdims=True)
        second = jnp.sum(jnp.where(lane >= HEAD_DIM, square, 0.0), axis=1, keepdims=True)
        return (jnp.max(first), jnp.max(second))

    @pl.when(block == 0)
    def prepare():
        lane = lanes_of(key_total)
        pair_keys = key_ref[0].astype(F32)
        keys = both_heads(lane, pair_keys, (key_bias(0, key_total, limit),))
        key_first[...] = keys[0].T
        key_second[...] = keys[1].T
        values = value_ref[0].astype(F32)
        value_first[...] = jnp.where(lane < HEAD_DIM, values, 1.0).astype(BF16)
        value_second[...] = jnp.where(lane >= HEAD_DIM, values, 1.0).astype(BF16)
        bounds = longest(lane, pair_keys)
        key_bound[0] = bounds[0]
        key_bound[1] = bounds[1]

    lane = lanes_of(block_rows)
    own = lane < HEAD_DIM
    scaled = query_ref[0].astype(F32) * HEAD_DIM ** (-0.5)
    queries = both_heads(lane, scaled, (1.0,))
    bounds = longest(lane, scaled)
    bound = jnp.maximum(bounds[0] * key_bound[0], bounds[1] * key_bound[1])
    sides = ((queries[0], key_first, value_first), (queries[1], key_second, value_second))

    def score_piece(head_queries, head_keys, piece):
        first_key, width, masked = piece
        scores = dot(head_queries, head_keys[:, first_key : first_key + width])
        if masked:
            row_pos = (
                query_start
                + block * block_rows
                + lax.broadcasted_iota(jnp.int32, (block_rows, width), 0)
            )
            key_pos = first_key + lax.broadcasted_iota(jnp.int32, (block_rows, width), 1)
            scores = jnp.where(key_pos <= row_pos, scores, NEGATIVE)
        return scores

    def store(sums, shifts):
        row_sum = pltpu.roll(jnp.where(own, sums[1], sums[0]), HEAD_DIM, 1)
        exact = jnp.where(own, sums[0], sums[1]) / row_sum
        exact_ref[0] = exact
        out_ref[0] = exact.astype(BF16)
        total_ref[0] = jnp.where(own, shifts[0], shifts[1]) + jnp.log(row_sum)

    def unshifted(pieces):
        units = [(piece, side) for piece in pieces for side in range(2)]

        def scores_of(unit):
            piece, side = unit
            return score_piece(sides[side][0], sides[side][1], piece)

        sums = [None, None]
        ahead = scores_of(units[0])
        for index, (piece, side) in enumerate(units):
            scores = ahead
            if index + 1 < len(units):
                ahead = scores_of(units[index + 1])
            weights = jnp.exp(scores).astype(BF16)
            term = dot(weights, sides[side][2][piece[0] : piece[0] + piece[1], :])
            sums[side] = term if sums[side] is None else sums[side] + term
        store(sums, (0.0, 0.0))

    def shifted(pieces):
        sums = []
        shifts = []
        for head_queries, head_keys, head_values in sides:
            scores = [score_piece(head_queries, head_keys, piece) for piece in pieces]
            row_max = None
            for part in scores:
                part_max = jnp.max(part, axis=1, keepdims=True)
                row_max = part_max if row_max is None else jnp.maximum(row_max, part_max)
            summed = None
            for piece, part in zip(pieces, scores):
                weights = jnp.exp(part - row_max).astype(BF16)
                term = dot(weights, head_values[piece[0] : piece[0] + piece[1], :])
                summed = term if summed is None else summed + term
            sums.append(summed)
            shifts.append(row_max)
        store(sums, shifts)

    def run(pieces):
        @pl.when(bound <= 1600.0)
        def plain():
            unshifted(pieces)

        @pl.when(bound > 1600.0)
        def general():
            shifted(pieces)

    def whole_row(masked):
        step = min(512, key_total)
        return [(first, step, masked) for first in range(0, key_total, step)]

    if not causal:
        run(whole_row(False))
    elif not aligned:
        run(whole_row(True))
    else:
        for index in range(key_total // block_rows):

            @pl.when(block == index)
            def one_block(index=index):
                first_key = index * block_rows
                pieces = [(0, first_key, False)] if index else []
                run(pieces + [(first_key, block_rows, True)])


def backward_kernel(
    causal,
    aligned,
    chunk_rows,
    scalars_ref,
    query_ref,
    key_ref,
    value_ref,
    grad_ref,
    exact_ref,
    total_ref,
    *refs,
):
    if len(refs) == 9:
        query_grad_ref, key_grad_ref = refs[:2]
        key_at = 0
    else:
        query_grad_ref = key_grad_ref = refs[0]
        key_at = PAIR
    (
        query_first,
        query_second,
        grad_first,
        grad_second,
        query_across,
        grad_across,
        query_sum,
    ) = refs[-7:]
    item = pl.program_id(0)
    block = pl.program_id(2)
    query_total = query_ref.shape[1]
    block_keys = key_ref.shape[1]
    limit = scalars_ref[1 + item]
    query_start = scalars_ref[0]
    scale = HEAD_DIM ** (-0.5)

    @pl.when(block == 0)
    def prepare():
        lane = lanes_of(query_total)
        own = lane < HEAD_DIM
        scaled = query_ref[0].astype(F32) * scale
        query_across[...] = scaled.astype(BF16).T
        total = -pltpu.roll(total_ref[0], HEAD_DIM, 1)
        queries = both_heads(lane, scaled, (1.0,) + three_parts(total))
        query_first[...] = queries[0]
        query_second[...] = queries[1]
        grads = grad_ref[0].astype(F32)
        grad_across[...] = grad_ref[0].T
        product = grads * exact_ref[0]
        first_sum = jnp.sum(jnp.where(own, product, 0.0), axis=1, keepdims=True)
        second_sum = jnp.sum(jnp.where(own, 0.0, product), axis=1, keepdims=True)
        weighted = -jnp.where(own, second_sum, first_sum)
        head_grads = both_heads(lane, grads, three_parts(weighted))
        grad_first[...] = head_grads[0]
        grad_second[...] = head_grads[1]
        query_sum[...] = jnp.zeros_like(query_sum)

    lane = lanes_of(block_keys)
    bias = key_bias(block * block_keys, block_keys, limit)
    pair_keys = key_ref[0].astype(F32)
    keys = [part.T for part in both_heads(lane, pair_keys, (bias, 1.0, 1.0, 1.0))]
    values = [
        part.T for part in both_heads(lane, value_ref[0].astype(F32), (1.0, 1.0, 1.0))
    ]
    keys_across = (pair_keys * scale).astype(BF16).T

    def run(pieces):
        key_parts = [None, None]
        value_parts = [None, None]
        units = [(piece, head) for piece in pieces for head in range(2)]
        sides = ((query_first, grad_first), (query_second, grad_second))

        def products_of(unit):
            (first_row, width, masked), head = unit
            rows = slice(first_row, first_row + width)
            scores = dot(sides[head][0][rows, :], keys[head])
            if masked:
                row_pos = (
                    query_start
                    + first_row
                    + lax.broadcasted_iota(jnp.int32, (width, block_keys), 0)
                )
                key_pos = block * block_keys + lax.broadcasted_iota(
                    jnp.int32, (width, block_keys), 1
                )
                scores = jnp.where(key_pos <= row_pos, scores, NEGATIVE)
            return (scores, dot(sides[head][1][rows, :], values[head]))

        ahead = products_of(units[0])
        for index, ((first_row, width, masked), head) in enumerate(units):
            scores, weight_grad = ahead
            if index + 1 < len(units):
                ahead = products_of(units[index + 1])
            rows = slice(first_row, first_row + width)
            head_rows = slice(head * HEAD_DIM, (head + 1) * HEAD_DIM)
            weights = jnp.exp(scores)
            score_grad = (weights * weight_grad).astype(BF16)
            value_term = dot(grad_across[head_rows, rows], weights.astype(BF16))
            key_term = dot(query_across[head_rows, rows], score_grad)
            query_sum[head_rows, rows] += matmul_back(keys_across[head_rows, :], score_grad)
            if key_parts[head] is None:
                key_parts[head], value_parts[head] = key_term, value_term
            else:
                key_parts[head] = key_parts[head] + key_term
                value_parts[head] = value_parts[head] + value_term
        block_rows = pl.ds(pl.multiple_of(block * block_keys, block_keys), block_keys)
        key_grad_ref[0, block_rows, key_at : key_at + PAIR] = (
            jnp.concatenate(key_parts, axis=0).T.astype(BF16)
        )
        key_grad_ref[0, block_rows, key_at + PAIR : key_at + 2 * PAIR] = (
            jnp.concatenate(value_parts, axis=0).T.astype(BF16)
        )

    def chunks(first_row, masked):
        return [
            (start, min(chunk_rows, query_total - start), masked)
            for start in range(first_row, query_total, chunk_rows)
        ]

    if not causal:
        run(chunks(0, False))
    elif not aligned:
        run(chunks(0, True))
    else:
        for index in range(query_total // block_keys):

            @pl.when(block == index)
            def one_block(index=index):
                first_row = index * block_keys
                run(
                    [(first_row, block_keys, True)]
                    + chunks(first_row + block_keys, False)
                )

    @pl.when(block == pl.num_programs(2) - 1)
    def finish():
        query_grad_ref[0, :, :PAIR] = query_sum[...].T.astype(BF16)


VMEM_BYTES = 56 * 1024 * 1024
SMALL_COST = pl.CostEstimate(flops=1000, bytes_accessed=1000, transcendentals=0)


def row_scale(values):
    return lax.rsqrt(jnp.mean(values * values, axis=1, keepdims=True) + EPSILON)


def norm_back(gradient, values, gain):
    inverse = row_scale(values)
    unit = values * inverse
    gain_grad = jnp.sum(gradient * unit, axis=0, keepdims=True)
    scaled = gradient * gain
    inner_mean = jnp.mean(scaled * unit, axis=1, keepdims=True)
    return (inverse * (scaled - unit * inner_mean), gain_grad)


def add_rows(total_ref, row):
    @pl.when(pl.program_id(0) == 0)
    def start():
        total_ref[...] = jnp.zeros_like(total_ref)

    total_ref[0:1, :] += row


def unpack_down(packed_ref, down_ref):
    for device in range(16):
        for group in range(8):
            for column in range(D // 256):
                row = (device * 8 + group) * 16
                down_ref[row : row + 16, column * 256 : (column + 1) * 256] = packed_ref[
                    device * 48 + column * 16 : device * 48 + (column + 1) * 16,
                    group * 256 : (group + 1) * 256,
                ]


def layer_forward_kernel(
    gain_row,
    next_row,
    attended_ref,
    start_ref,
    gate_up_ref,
    packed_ref,
    output_ref,
    gains_ref,
    middle_ref,
    normed_ref,
    slopes_ref,
    hidden_ref,
    rounded_ref,
    *refs,
):
    rows_ref, down_ref = refs[-2:]

    @pl.when(pl.program_id(0) == 0)
    def unpack():
        unpack_down(packed_ref, down_ref)

    middle = start_ref[...].astype(F32) + dot(attended_ref[...], output_ref[...])
    middle_ref[...] = middle
    normed = (middle * row_scale(middle) * gains_ref[gain_row : gain_row + 1, :]).astype(BF16)
    normed_ref[...] = normed.T

    span = 2 * FF_BLOCK

    def product_of(first):
        return dot(normed, gate_up_ref[:, 2 * first : 2 * (first + span)])

    ahead = product_of(0)
    for start in range(0, FF, span):
        product = ahead
        if start + span < FF:
            ahead = product_of(start + span)
        for first in range(start, start + span, FF_BLOCK):
            both = product[:, 2 * (first - start) : 2 * (first - start + FF_BLOCK)]
            gate, up = both[:, :FF_BLOCK], both[:, FF_BLOCK:]
            square = gate * gate
            bend = jnp.tanh(gate * (GELU_SCALE + (GELU_SCALE * GELU_CUBE) * square))
            half = 0.5 + 0.5 * bend
            bent = gate * half
            slope = half + (1.0 - bend * bend) * (
                gate * (0.5 * GELU_SCALE + (1.5 * GELU_SCALE * GELU_CUBE) * square)
            )
            slopes_ref[:, 2 * first : 2 * first + FF_BLOCK] = (up * slope).astype(BF16)
            slopes_ref[:, 2 * first + FF_BLOCK : 2 * (first + FF_BLOCK)] = bent.astype(BF16)
            hidden = (bent * up).astype(BF16)
            rows_ref[:, first : first + FF_BLOCK] = hidden
            hidden_ref[first : first + FF_BLOCK, :] = hidden.T
    final = middle + dot(rows_ref[...], down_ref[...])
    rounded_ref[...] = final.astype(BF16)
    if next_row is not None:
        refs[0][...] = final
        next_normed = (
            final * row_scale(final) * gains_ref[next_row : next_row + 1, :]
        ).astype(BF16)
        refs[1][...] = next_normed
        refs[2][...] = next_normed.T


def layer_backward_kernel(
    gain_row,
    grad_ref,
    slopes_ref,
    middle_ref,
    gate_up_ref,
    packed_ref,
    output_ref,
    gains_ref,
    gate_grad_ref,
    middle_grad_ref,
    rounded_ref,
    head_grad_ref,
    gain_grad_ref,
    down_ref,
):
    @pl.when(pl.program_id(0) == 0)
    def unpack():
        unpack_down(packed_ref, down_ref)

    out_grad = grad_ref[...].astype(BF16)

    span = 2 * FF_BLOCK

    def product_of(first):
        return matmul_back(out_grad, down_ref[first : first + span, :])

    ahead = product_of(0)
    for start in range(0, FF, span):
        product = ahead
        if start + span < FF:
            ahead = product_of(start + span)
        for first in range(start, start + span, FF_BLOCK):
            both = slice(2 * first, 2 * (first + FF_BLOCK))
            hidden_grad = product[:, first - start : first - start + FF_BLOCK]
            hidden_grad = jnp.concatenate([hidden_grad, hidden_grad], axis=1)
            gate_grad_ref[:, both] = (hidden_grad * slopes_ref[:, both].astype(F32)).astype(BF16)
    normed_grad = matmul_back(gate_grad_ref[...], gate_up_ref[...])
    in_grad, gain_grad = norm_back(
        normed_grad, middle_ref[...], gains_ref[gain_row : gain_row + 1, :]
    )
    add_rows(gain_grad_ref, gain_grad)
    middle_grad = grad_ref[...].astype(F32) + in_grad
    middle_grad_ref[...] = middle_grad
    rounded = middle_grad.astype(BF16)
    rounded_ref[...] = rounded
    head_grad_ref[...] = matmul_back(rounded, output_ref[...]).astype(BF16)


def project_back_kernel(gain_row, sides, with_rounded, with_head, *refs):
    grads, weights = refs[:sides], refs[sides : 2 * sides]
    base_ref, values_ref, gains_ref = refs[2 * sides : 2 * sides + 3]
    outs = list(refs[2 * sides + 3 :])
    output_ref = outs.pop(0) if with_head else None
    normed_grad = None
    for grad_ref, weight_ref in zip(grads, weights):
        term = matmul_back(grad_ref[...], weight_ref[...])
        normed_grad = term if normed_grad is None else normed_grad + term
    in_grad, gain_grad = norm_back(
        normed_grad, values_ref[...].astype(F32), gains_ref[gain_row : gain_row + 1, :]
    )
    total = base_ref[...].astype(F32) + in_grad
    outs[0][...] = total
    add_rows(outs[1], gain_grad)
    if with_rounded:
        rounded = total.astype(BF16)
        outs[2][...] = rounded
        if with_head:
            outs[3][...] = matmul_back(rounded, output_ref[...]).astype(BF16)


def rows_call(kernel, rows, operands, outs, scratch, name):
    step = min(512, rows)
    in_specs = []
    for array, stays in operands:
        if stays is None:
            in_specs.append(pl.BlockSpec((step, array.shape[1]), lambda m: (m, 0)))
        else:
            width, column = stays
            in_specs.append(
                pl.BlockSpec(
                    (array.shape[0], width),
                    functools.partial(lambda at, m: (0, at), column // width),
                    pipeline_mode=pl.Buffered(1),
                )
            )
    out_specs = []
    out_shape = []
    for width, dtype, *across in outs:
        if across:
            out_specs.append(pl.BlockSpec((width, step), lambda m: (0, m)))
            out_shape.append(jax.ShapeDtypeStruct((width, rows), dtype))
        elif dtype is None:
            out_specs.append(pl.BlockSpec((8, width), lambda m: (0, 0)))
            out_shape.append(jax.ShapeDtypeStruct((8, width), F32))
        else:
            out_specs.append(pl.BlockSpec((step, width), lambda m: (m, 0)))
            out_shape.append(jax.ShapeDtypeStruct((rows, width), dtype))
    return pl.pallas_call(
        kernel,
        grid=(rows // step,),
        in_specs=in_specs,
        out_specs=out_specs,
        out_shape=out_shape,
        scratch_shapes=scratch,
        compiler_params=pltpu.CompilerParams(vmem_limit_bytes=VMEM_BYTES),
        cost_estimate=SMALL_COST,
        name=name,
    )(*[array for array, stays in operands])


LAYER_SIDES = ((2 * FF, 0), (FF, 2 * FF), (D, 3 * FF))


def layer_forward(attended, start, layer, gains, gain_row, next_row=None):
    outs = [(D, F32), (D, BF16, True), (2 * FF, BF16), (FF, BF16, True), (D, BF16)]
    if next_row is not None:
        outs += [(D, F32), (D, BF16), (D, BF16, True)]
    return rows_call(
        functools.partial(layer_forward_kernel, gain_row, next_row),
        attended.shape[0],
        [(attended, None), (start, None)]
        + [(layer, side) for side in LAYER_SIDES]
        + [(gains, (D, 0))],
        outs,
        [pltpu.VMEM((min(512, attended.shape[0]), FF), BF16), pltpu.VMEM((FF, D), BF16)],
        "layer_forward",
    )


def layer_backward(grad, slopes, middle, layer, gains, gain_row):
    return rows_call(
        functools.partial(layer_backward_kernel, gain_row),
        grad.shape[0],
        [(grad, None), (slopes, None), (middle, None)]
        + [(layer, side) for side in LAYER_SIDES]
        + [(gains, (D, 0))],
        [(2 * FF, BF16), (D, F32), (D, BF16), (D, BF16), (D, None)],
        [pltpu.VMEM((FF, D), BF16)],
        "layer_backward",
    )


def project_back(sides, base, values, gains, gain_row, rounded=False, output=None):
    operands = [(grad, None) for grad, weight, place in sides]
    operands += [(weight, place) for grad, weight, place in sides]
    operands += [(base, None), (values, None), (gains, (D, 0))]
    outs = [(D, F32), (D, None)]
    if rounded:
        outs.append((D, BF16))
    if output is not None:
        operands.append(output)
        outs.append((D, BF16))
    return rows_call(
        functools.partial(
            project_back_kernel, gain_row, len(sides), rounded, output is not None
        ),
        base.shape[0],
        operands,
        outs,
        [],
        "project_back",
    )


def weight_grad_kernel(left_ref, right_ref, *refs):
    out_ref, across = refs[-2:]

    @pl.when(pl.program_id(0) == 0)
    def turn():
        step = min(256, left_ref.shape[0])
        for first_row in range(0, left_ref.shape[0], step):
            across[:, first_row : first_row + step] = left_ref[first_row : first_row + step, :].T

    out_ref[...] = dot(across[...], right_ref[...]).astype(BF16)


def turned_grad_kernel(left_ref, right_ref, *refs):
    refs[-1][...] = dot(left_ref[...], right_ref[...]).astype(BF16)


def turn_kernel(rows_ref, out_ref):
    out_ref[...] = rows_ref[...].T


def turn_rows(array):
    return rows_call(
        turn_kernel, array.shape[0], [(array, None)], [(array.shape[1], BF16, True)], [], "turn_rows"
    )[0]


def down_grad_kernel(shard_rows, hidden_ref, right_ref, *refs):
    out_ref = refs[-1]
    term = dot(hidden_ref[...], right_ref[...]).astype(BF16)
    group_rows = FF * shard_rows // D // 8
    for device in range(out_ref.shape[0] // shard_rows):
        for column in range(D // 256):
            for group in range(8):
                first_row = (device * 8 + group) * group_rows
                out_row = device * shard_rows + column * group_rows
                out_ref[out_row : out_row + group_rows, group * 256 : (group + 1) * 256] = term[
                    first_row : first_row + group_rows, column * 256 : (column + 1) * 256
                ]


def fill_call(kernel, grid, in_specs, out_spec, columns, scratch, operands, buffer, name):
    operands = list(operands)
    in_specs = list(in_specs)
    aliases = {}
    if buffer is not None:
        aliases = {len(operands): 0}
        operands.append(buffer)
        in_specs.append(pl.BlockSpec(memory_space=pl.ANY))
    return pl.pallas_call(
        kernel,
        grid=grid,
        in_specs=in_specs,
        out_specs=out_spec,
        out_shape=jax.ShapeDtypeStruct((D, columns), BF16),
        scratch_shapes=scratch,
        input_output_aliases=aliases,
        compiler_params=pltpu.CompilerParams(vmem_limit_bytes=VMEM_BYTES),
        cost_estimate=SMALL_COST,
        name=name,
    )(*operands)


def fill_weight_grad(buffer, columns, first_column, left_side, right_side, turned=False):
    rows = right_side.shape[0]
    step = 1024 if right_side.shape[1] % 1024 == 0 else D
    first_step = first_column // step
    return fill_call(
        turned_grad_kernel if turned else weight_grad_kernel,
        (right_side.shape[1] // step,),
        [
            pl.BlockSpec(left_side.shape, lambda n: (0, 0)),
            pl.BlockSpec((rows, step), lambda n: (0, n)),
        ],
        pl.BlockSpec((D, step), lambda n: (0, first_step + n)),
        columns,
        [] if turned else [pltpu.VMEM((D, rows), BF16)],
        (left_side, right_side),
        buffer,
        "weight_grad",
    )


def fill_down_grad(buffer, columns, first_column, shard_rows, hidden, out_grad):
    rows = out_grad.shape[0]
    wide = D // shard_rows
    if FF // wide // 8 % 16:
        cut = matmul(hidden, out_grad).astype(BF16).reshape(wide, 8, FF // wide // 8, 3, 256)
        cut = cut.transpose(0, 3, 2, 1, 4).reshape(D, FF)
        return lax.dynamic_update_slice(buffer, cut, (0, first_column))
    devices = math.gcd(wide, 4)
    first_step = first_column // FF
    return fill_call(
        functools.partial(down_grad_kernel, shard_rows),
        (wide // devices,),
        [
            pl.BlockSpec((devices * FF // wide, rows), lambda n: (n, 0)),
            pl.BlockSpec((rows, D), lambda n: (0, 0)),
        ],
        pl.BlockSpec((devices * shard_rows, FF), lambda n: (n, first_step)),
        columns,
        [],
        (hidden, out_grad),
        buffer,
        "down_grad",
    )


def attend_forward(query_side, key_side, value_side, scalars, causal, aligned):
    (query_array, query_at), (key_array, key_at), (value_array, value_at) = (
        query_side,
        key_side,
        value_side,
    )
    query_step, key_step = query_array.shape[2] // D, key_array.shape[2] // D
    items, rows = query_array.shape[0], query_array.shape[1]
    keys = key_array.shape[1]
    block_rows = min(512 if causal else 1024, rows)
    return pl.pallas_call(
        functools.partial(forward_kernel, causal, aligned),
        grid=(items, PAIRS, rows // block_rows),
        in_specs=[
            pl.BlockSpec(memory_space=pltpu.SMEM),
            pl.BlockSpec((1, block_rows, PAIR), lambda i, p, b: (i, b, query_at + query_step * p)),
            pl.BlockSpec((1, keys, PAIR), lambda i, p, b: (i, 0, key_at + key_step * p)),
            pl.BlockSpec((1, keys, PAIR), lambda i, p, b: (i, 0, value_at + key_step * p)),
        ],
        out_specs=[
            pl.BlockSpec((1, block_rows, PAIR), lambda i, p, b: (i, b, p)),
            pl.BlockSpec((1, block_rows, PAIR), lambda i, p, b: (i, b, p)),
            pl.BlockSpec((1, block_rows, PAIR), lambda i, p, b: (i, b, p)),
        ],
        out_shape=[
            jax.ShapeDtypeStruct((items, rows, D), BF16),
            jax.ShapeDtypeStruct((items, rows, D), F32),
            jax.ShapeDtypeStruct((items, rows, D), F32),
        ],
        scratch_shapes=[
            pltpu.VMEM((PAIR, keys), BF16),
            pltpu.VMEM((PAIR, keys), BF16),
            pltpu.VMEM((keys, PAIR), BF16),
            pltpu.VMEM((keys, PAIR), BF16),
            pltpu.SMEM((2,), F32),
        ],
        compiler_params=pltpu.CompilerParams(vmem_limit_bytes=VMEM_BYTES),
        cost_estimate=SMALL_COST,
        name="attend_forward",
    )(scalars, query_array, key_array, value_array)


def attend_backward(
    query_side,
    key_side,
    value_side,
    head_grad,
    exact,
    total,
    scalars,
    causal,
    aligned,
    first_pair=0,
    pairs=PAIRS,
    block_keys=512,
    chunk_rows=1024,
):
    (query_array, query_at), (key_array, key_at), (value_array, value_at) = (
        query_side,
        key_side,
        value_side,
    )
    query_step, key_step = query_array.shape[2] // D, key_array.shape[2] // D
    items, rows = query_array.shape[0], query_array.shape[1]
    keys = key_array.shape[1]
    chunk_rows = min(chunk_rows, rows)
    whole = pl.BlockSpec((1, rows, PAIR), lambda i, p, b: (i, 0, first_pair + p))
    together = query_array is key_array
    if together:
        widths = ((rows, 3 * PAIR),)
    else:
        widths = ((rows, PAIR), (keys, 2 * PAIR))
    return pl.pallas_call(
        functools.partial(backward_kernel, causal, aligned, chunk_rows),
        grid=(items, pairs, keys // block_keys),
        in_specs=[
            pl.BlockSpec(memory_space=pltpu.SMEM),
            pl.BlockSpec((1, rows, PAIR), lambda i, p, b: (i, 0, query_at + query_step * (first_pair + p))),
            pl.BlockSpec((1, block_keys, PAIR), lambda i, p, b: (i, b, key_at + key_step * (first_pair + p))),
            pl.BlockSpec((1, block_keys, PAIR), lambda i, p, b: (i, b, value_at + key_step * (first_pair + p))),
            whole,
            whole,
            whole,
        ],
        out_specs=[pl.BlockSpec((1,) + width, lambda i, p, b: (i, 0, p)) for width in widths],
        out_shape=[
            jax.ShapeDtypeStruct((items, width[0], width[1] * pairs), BF16) for width in widths
        ],
        scratch_shapes=[
            pltpu.VMEM((rows, PAIR), BF16),
            pltpu.VMEM((rows, PAIR), BF16),
            pltpu.VMEM((rows, PAIR), BF16),
            pltpu.VMEM((rows, PAIR), BF16),
            pltpu.VMEM((PAIR, rows), BF16),
            pltpu.VMEM((PAIR, rows), BF16),
            pltpu.VMEM((PAIR, rows), F32),
        ],
        compiler_params=pltpu.CompilerParams(vmem_limit_bytes=VMEM_BYTES),
        cost_estimate=SMALL_COST,
        name="attend_backward",
    )(scalars, query_array, key_array, value_array, head_grad, exact, total)


def in_order(first, second):
    return lax.optimization_barrier((first, second))


def on_device(
    narrow,
    patch_input,
    text_input,
    patch_cotangent,
    text_cotangent,
    patch_count,
    header_len,
    text_len,
    norm_gains,
    header_embed,
    enc_project,
    enc_output,
    enc_gate_up,
    enc_down,
    self_project,
    self_output,
    cross_project,
    cross_output,
    dec_gate_up,
    dec_down,
):
    swapped = narrow == 2 and patch_input.shape[0] == 2
    spot = lax.axis_index("narrow")
    shard_rows = norm_gains.shape[0]
    wide = D // shard_rows

    def partner(array):
        return lax.ppermute(array, "narrow", [(0, 1), (1, 0)])

    def pick(own, got, position):
        slot = jnp.arange(2, dtype=jnp.int32).reshape(2, 1, 1)
        return jnp.where(slot == position, own[None], got[None])

    def take_items(array):
        if not swapped:
            return array
        own = lax.dynamic_index_in_dim(array, spot, 0, keepdims=False)
        got = partner(lax.dynamic_index_in_dim(array, 1 - spot, 0, keepdims=False))
        return pick(own, got, spot).reshape(1, -1, D)

    def halve_rows(array):
        half = array.shape[1] // 2
        own = lax.dynamic_slice_in_dim(array[0], spot * half, half, 0)
        away = lax.dynamic_slice_in_dim(array[0], (1 - spot) * half, half, 0)
        return (own, away.astype(BF16))

    def send_rows(array, tied=None):
        if not swapped:
            return (array, None), tied
        own, away = halve_rows(array)
        away, tied = in_order(away, tied)
        return (own, partner(away)), tied

    def place_rows(sent):
        own, got = sent
        return own if got is None else pick(own, got.astype(own.dtype), spot)

    def gather(*arrays):
        whole = jnp.concatenate(arrays, axis=1) if len(arrays) > 1 else arrays[0]
        return lax.all_gather(whole, "wide", axis=0, tiled=True)

    def scatter(summed):
        return lax.psum_scatter(summed, "wide", scatter_dimension=0, tiled=True)

    def sum_small(array):
        step = 1
        while step < wide:
            ways = min(4, wide // step)
            got = [
                lax.ppermute(
                    array, "wide", [(index, index ^ (step * way)) for index in range(wide)]
                )
                for way in range(1, ways)
            ]
            array = functools.reduce(jnp.add, got, array)
            step *= ways
        return array

    def exchange(summed):
        return partner(summed) if narrow == 2 else None

    def finish(summed, widths, got=None):
        if narrow == 2:
            got = exchange(summed) if got is None else got
            total = summed.astype(F32) + got.astype(F32)
        else:
            total = lax.psum(summed, "narrow").astype(F32)
        parts = []
        start = 0
        for width in widths:
            parts.append(total[:, start : start + width])
            start += width
        return parts

    def gather_layer(gate_up, down, output, *more):
        if FF // wide == 128:
            packed = down.reshape(8, 16, D // 256, 256).transpose(2, 1, 0, 3).reshape(-1, FF)
            return gather(gate_up, packed, output, *more)
        packed = gather(down).reshape(16, 8, 16, D // 256, 256)
        packed = packed.transpose(0, 3, 2, 1, 4).reshape(D, FF)
        return jnp.concatenate([gather(gate_up), packed, gather(output, *more)], axis=1)

    groups = 8
    group_rows = FF // wide // groups

    def rows_to_down(array):
        cut = array.reshape(-1, D // 256, group_rows, groups, 256)
        return cut.transpose(0, 3, 2, 1, 4).reshape(-1, D)

    def by_pair(array):
        sides = array.shape[1] // D
        return array.reshape(-1, sides, PAIRS, PAIR).swapaxes(1, 2).reshape(array.shape)

    def by_side(array):
        sides = array.shape[1] // D
        return array.reshape(-1, PAIRS, sides, PAIR).swapaxes(1, 2).reshape(array.shape)

    def by_block(array):
        return array.reshape(-1, 2, FF // FF_BLOCK, FF_BLOCK).swapaxes(1, 2).reshape(array.shape)

    def by_half(array):
        return array.reshape(-1, FF // FF_BLOCK, 2, FF_BLOCK).swapaxes(1, 2).reshape(array.shape)

    enc_project, self_project = by_pair(enc_project), by_pair(self_project)
    cross_project = jnp.concatenate([cross_project[:, :D], by_pair(cross_project[:, D:])], axis=1)
    enc_gate_up, dec_gate_up = by_block(enc_gate_up), by_block(dec_gate_up)
    small = jnp.concatenate(
        [norm_gains, header_embed[:, None], jnp.zeros((shard_rows, 121), BF16)], axis=1
    )
    patch_rows_in = take_items(patch_input)
    first_group = gather(enc_project, small)
    second_group = gather_layer(enc_gate_up, enc_down, enc_output, self_project)
    third_group = gather(cross_project[:, D:], cross_project[:, :D], self_output)
    small_all = first_group[:, 3 * D :]
    cross_memory_at = (2 * D, 0)
    cross_query_at = (D, 2 * D)
    self_project_at = (3 * D, 3 * FF + D)
    self_output_at = (D, 3 * D)

    def part_of(array, place):
        return array[:, place[1] : place[1] + place[0]]

    items, patch_rows = patch_rows_in.shape[0], patch_rows_in.shape[1]
    text_rows = text_input.shape[1] * (2 if swapped else 1)
    if swapped:
        patch_total = lax.dynamic_slice_in_dim(patch_count, spot, 1)
        header_total = lax.dynamic_slice_in_dim(header_len, spot, 1)
        text_total = lax.dynamic_slice_in_dim(text_len, spot, 1)
        patch_first = jnp.int32(0)
        text_first = jnp.int32(0)
    else:
        patch_total, header_total, text_total = patch_count, header_len, text_len
        patch_first = spot * patch_rows
        text_first = spot * text_rows
    patch_scalars = jnp.concatenate([patch_first[None], patch_total])
    cross_scalars = jnp.concatenate([text_first[None], patch_total])
    text_scalars = jnp.concatenate([text_first[None], text_total])
    patch_flat = items * patch_rows
    text_flat = items * text_rows

    def all_keys(array):
        return array if swapped else lax.all_gather(array, "narrow", axis=1, tiled=True)

    def own_keys(array):
        if swapped:
            return array
        return lax.psum_scatter(array, "narrow", scatter_dimension=1, tiled=True)

    def split_of(projected):
        if swapped:
            return ((projected, 0), (projected, 1), (projected, 2))
        shape = projected.shape[:2]
        by_pair = projected.reshape(shape + (PAIRS, 3 * PAIR))
        keys = all_keys(by_pair[:, :, :, PAIR:].reshape(shape + (2 * D,)))
        return ((by_pair[:, :, :, :PAIR].reshape(shape + (D,)), 0), (keys, 0), (keys, 1))

    def joined(grads):
        if swapped:
            return grads[0].reshape(-1, grads[0].shape[2])
        query_grad, key_grad = grads[0], own_keys(grads[1])
        pairs = query_grad.shape[2] // PAIR
        shape = query_grad.shape[:2] + (pairs, -1)
        return jnp.concatenate(
            [query_grad.reshape(shape), key_grad.reshape(shape)], axis=3
        ).reshape(-1, 3 * pairs * PAIR)

    gains = small_all[:, :8].astype(F32).T
    header_full = gains[6]

    patch_pos = patch_first + jnp.arange(patch_rows, dtype=jnp.int32)
    header_mask = (
        (patch_pos[None, :] < header_total[:, None]).astype(F32).reshape(patch_flat, 1)
    )
    patch_start = patch_rows_in.astype(F32).reshape(patch_flat, D) + header_mask * header_full
    patch_start, (text_input, patch_cotangent, text_cotangent) = in_order(
        patch_start, (text_input, patch_cotangent, text_cotangent)
    )
    text_rows_in = take_items(text_input)
    patch_grad_in = take_items(patch_cotangent)
    text_grad_in = take_items(text_cotangent)
    attn_input = rms_norm(patch_start, gains[0])
    enc_qkv = (
        matmul(attn_input, first_group[:, : 3 * D])
        .astype(BF16)
        .reshape(items, patch_rows, 3 * D)
    )
    enc_sides = split_of(enc_qkv)
    enc_attended, enc_exact, enc_total = attend_forward(*enc_sides, patch_scalars, False, swapped)
    attn_input, enc_attended = in_order(attn_input, enc_attended)
    attn_turned = turn_rows(attn_input)
    (text_rows_in, patch_grad_in, text_grad_in, attn_turned), enc_attended = in_order(
        (text_rows_in, patch_grad_in, text_grad_in, attn_turned), enc_attended
    )
    enc_attended_flat = enc_attended.reshape(patch_flat, D)
    (
        patch_middle,
        mlp_input,
        enc_slopes,
        enc_hidden,
        patch_rounded,
        patch_final,
        memory_input,
        memory_turned,
    ) = layer_forward(enc_attended_flat, patch_start, second_group, gains, 1, 4)
    memory_input, (cross_output, dec_gate_up, dec_down) = in_order(
        memory_input, (cross_output, dec_gate_up, dec_down)
    )
    fourth_group = gather_layer(dec_gate_up, dec_down, cross_output)
    patch_sent, unused = send_rows(patch_rounded.reshape(items, patch_rows, D))

    text_start = text_rows_in.reshape(text_flat, D)
    self_input = rms_norm(text_start.astype(F32), gains[2])
    self_qkv = (
        matmul(self_input, part_of(second_group, self_project_at))
        .astype(BF16)
        .reshape(items, text_rows, 3 * D)
    )
    self_sides = split_of(self_qkv)
    self_attended, self_exact, self_total = attend_forward(*self_sides, text_scalars, True, swapped)
    self_attended_flat = self_attended.reshape(text_flat, D)
    text_middle = text_start.astype(F32) + matmul(
        self_attended_flat, part_of(third_group, self_output_at)
    )
    cross_input = rms_norm(text_middle, gains[3])
    cross_queries = (
        matmul(cross_input, part_of(third_group, cross_query_at))
        .astype(BF16)
        .reshape(items, text_rows, D)
    )
    memory_kv = all_keys(
        matmul(memory_input, part_of(third_group, cross_memory_at))
        .astype(BF16)
        .reshape(items, patch_rows, 2 * D)
    )
    cross_sides = ((cross_queries, 0), (memory_kv, 0), (memory_kv, 1))
    cross_attended, cross_exact, cross_total = attend_forward(*cross_sides, cross_scalars, False, swapped)
    cross_attended_flat = cross_attended.reshape(text_flat, D)
    patch_sent, cross_attended_flat = in_order(patch_sent, cross_attended_flat)
    text_late, ffn_input, ffn_slopes, ffn_hidden, text_rounded = layer_forward(
        cross_attended_flat, text_middle, fourth_group, gains, 5
    )
    text_sent, unused = send_rows(text_rounded.reshape(items, text_rows, D))

    ffn_out_grad = text_grad_in.reshape(text_flat, D)
    ffn_gate_grad, late_grad, cross_out_grad, cross_head_grad, gain_ffn = layer_backward(
        ffn_out_grad, ffn_slopes, text_late, fourth_group, gains, 5
    )
    cross_head_grad = cross_head_grad.reshape(items, text_rows, D)
    first_width = 2 * FF + FF
    first_terms = fill_weight_grad(None, first_width, 0, ffn_input, ffn_gate_grad, True)
    first_terms = fill_down_grad(
        first_terms, first_width, 2 * FF, shard_rows, ffn_hidden, ffn_out_grad
    )
    first_terms, (cross_out_grad, cross_head_grad) = in_order(
        first_terms, (cross_out_grad, cross_head_grad)
    )
    first_sum = scatter(first_terms)

    second_width = 4 * D
    second_terms = fill_weight_grad(None, second_width, 0, cross_attended_flat, cross_out_grad)
    query_grad, key_grad = attend_backward(
        *cross_sides,
        cross_head_grad,
        cross_exact,
        cross_total,
        cross_scalars,
        False,
        swapped,
    )
    cross_query_grad = query_grad.reshape(text_flat, D)
    memory_kv_grad = own_keys(key_grad).reshape(patch_flat, 2 * D)
    second_terms = fill_weight_grad(second_terms, second_width, D, cross_input, cross_query_grad)
    second_terms = fill_weight_grad(
        second_terms, second_width, 2 * D, memory_turned, memory_kv_grad, True
    )
    second_terms, (cross_query_grad, memory_kv_grad) = in_order(
        second_terms, (cross_query_grad, memory_kv_grad)
    )
    second_sum = scatter(second_terms)
    middle_grad, gain_cross, self_out_grad, self_head_grad = project_back(
        [(cross_query_grad, third_group, cross_query_at)],
        late_grad,
        text_middle,
        gains,
        3,
        True,
        (third_group, self_output_at),
    )
    self_head_grad = self_head_grad.reshape(items, text_rows, D)

    self_terms = fill_weight_grad(None, second_width, 0, self_attended_flat, self_out_grad)
    self_qkv_grad = joined(
        attend_backward(
            *self_sides, self_head_grad, self_exact, self_total, text_scalars, True, swapped
        )
    )
    self_terms = fill_weight_grad(self_terms, second_width, D, self_input, self_qkv_grad)
    (self_terms, first_sum, text_sent), (self_qkv_grad, memory_kv_grad) = in_order(
        (self_terms, first_sum, text_sent), (self_qkv_grad, memory_kv_grad)
    )
    self_sum = scatter(self_terms)

    patch_grad, gain_memory, down_grad = project_back(
        [(memory_kv_grad, third_group, cross_memory_at)],
        patch_grad_in.reshape(patch_flat, D),
        patch_final,
        gains,
        4,
        True,
    )
    enc_gate_grad, enc_middle_grad, enc_out_grad, enc_head_grad, gain_mlp = layer_backward(
        patch_grad, enc_slopes, patch_middle, second_group, gains, 1
    )
    enc_head_grad = enc_head_grad.reshape(items, patch_rows, D)
    third_width = 2 * FF + FF
    third_terms = fill_weight_grad(None, third_width, 0, mlp_input, enc_gate_grad, True)
    third_terms = fill_down_grad(
        third_terms, third_width, 2 * FF, shard_rows, enc_hidden, down_grad
    )
    (third_terms, second_sum), (enc_out_grad, enc_head_grad) = in_order(
        (third_terms, second_sum), (enc_out_grad, enc_head_grad)
    )
    third_sum = scatter(third_terms)
    fourth_width = D + 3 * D
    fourth_terms = fill_weight_grad(None, fourth_width, 0, enc_attended_flat, enc_out_grad)
    grad_dec_gate_up, grad_dec_down = finish(first_sum, (2 * FF, FF))
    grad_cross_output, grad_cross_query, grad_memory_kv = finish(second_sum, (D, D, 2 * D))
    text_back, gain_self = project_back(
        [(self_qkv_grad, second_group, self_project_at)], middle_grad, text_start, gains, 2
    )
    text_back_sent, unused = send_rows(text_back.reshape(items, text_rows, D))
    fourth_terms, enc_head_grad = in_order(fourth_terms, enc_head_grad)

    enc_qkv_grad = joined(
        attend_backward(
            *enc_sides, enc_head_grad, enc_exact, enc_total, patch_scalars, False, swapped
        )
    )
    late = (
        text_back_sent,
        gain_self,
        self_sum,
        third_sum,
        grad_dec_gate_up,
        grad_dec_down,
        grad_cross_output,
        grad_cross_query,
        grad_memory_kv,
    )
    late, enc_qkv_grad = in_order(late, enc_qkv_grad)
    (
        text_back_sent,
        gain_self,
        self_sum,
        third_sum,
        grad_dec_gate_up,
        grad_dec_down,
        grad_cross_output,
        grad_cross_query,
        grad_memory_kv,
    ) = late
    fourth_terms = fill_weight_grad(
        fourth_terms, fourth_width, D, attn_turned, enc_qkv_grad, True
    )
    fourth_terms, enc_qkv_grad = in_order(fourth_terms, enc_qkv_grad)
    fourth_sum = scatter(fourth_terms)
    self_got, third_got = exchange(self_sum), exchange(third_sum)
    (self_got, third_got), enc_qkv_grad = in_order((self_got, third_got), enc_qkv_grad)

    start_grad, gain_attn = project_back(
        [(enc_qkv_grad, first_group, (3 * D, 0))], enc_middle_grad, patch_start, gains, 0
    )
    patch_back_sent, start_grad = send_rows(
        start_grad.reshape(items, patch_rows, D), start_grad
    )
    header_term = jnp.sum(start_grad * header_mask, axis=0, keepdims=True)
    terms = (gain_attn, gain_mlp, gain_self, gain_cross, gain_memory, gain_ffn, header_term)
    small_term = jnp.concatenate([term[:1] for term in terms + (jnp.zeros_like(header_term),)])
    small_own = lax.dynamic_slice_in_dim(
        sum_small(small_term), lax.axis_index("wide") * shard_rows, shard_rows, 1
    ).T
    small_own = jnp.pad(small_own.astype(BF16), ((0, 0), (0, PAIR - small_own.shape[1])))

    grad_self_output, grad_self_project = finish(self_sum, (D, 3 * D), self_got)
    grad_enc_gate_up, grad_enc_down = finish(third_sum, (2 * FF, FF), third_got)
    grad_enc_output, grad_enc_project, grad_small = finish(
        jnp.concatenate([fourth_sum, small_own], axis=1), (D, 3 * D, PAIR)
    )
    patch_output = place_rows(patch_sent)
    text_output = place_rows(text_sent)
    text_input_grad = place_rows(text_back_sent)
    patch_input_grad = place_rows(patch_back_sent)
    grad_cross_project = jnp.concatenate([grad_cross_query, by_side(grad_memory_kv)], axis=1)
    return (
        patch_output,
        text_output,
        patch_input_grad,
        text_input_grad,
        grad_small[:, :6],
        grad_small[:, 6],
        by_side(grad_enc_project),
        grad_enc_output,
        by_half(grad_enc_gate_up),
        rows_to_down(grad_enc_down),
        by_side(grad_self_project),
        grad_self_output,
        grad_cross_project,
        grad_cross_output,
        by_half(grad_dec_gate_up),
        rows_to_down(grad_dec_down),
    )


def solution(mesh):
    rows = P("wide", "narrow", None)
    weight = P("wide", None)
    vector = P("wide")
    return jax.shard_map(
        functools.partial(on_device, mesh.shape["narrow"]),
        mesh=mesh,
        in_specs=(rows,) * 4 + (vector,) * 3 + (weight, vector) + (weight,) * 10,
        out_specs=(rows,) * 4 + (weight, vector) + (weight,) * 10,
        check_vma=False,
    )
```

time: 3720 us -> 929 us (0.25)
  matrix products: 1910 us -> 30.4 us
  Pallas kernels: 0 us -> 674 us
  waiting for transfers between devices: 707 us -> 54.8 us
  other arithmetic: 538 us -> 40.8 us
  local copies, waits for them, and re-layouts: 428 us -> 81.4 us
  blocking collectives: 88.4 us -> 0 us
    dot_general x393 -> x5, matrix products: 1910 us -> 30.4 us  [matmul(): return jnp.dot(left_side, right_side, preferred_element_type=F32)]
    pallas_call x0 -> x26, Pallas kernels: none -> 674 us  [the longest x3 254 us: attend_backward(): pl.pallas_call(functools.partial(backward_kernel, causal, aligned, chunk_...]
    reduce_scatter x22 -> x5, waiting for transfers between devices: 596 us -> 0.02 us  [scatter(): return lax.psum_scatter(summed, 'wide', scatter_dimension=0, tiled=True)]
    reduce_sum x43 -> x3, other arithmetic: 228 us -> 4.19 us  [the longest x1 3.33 us: on_device(): header_term = jnp.sum(start_grad * header_mask, axis=0, keepdims=True)]
    lt x160 -> x0, other arithmetic: 203 us -> none  [block_scores(): key_pos[None, :] < key_limit]
    while x312 -> x0, local copies, waits for them, and re-layouts: 111 us -> none
    unnamed x329 -> x118, local copies, waits for them, and re-layouts: 124 us -> 16.3 us
    dynamic_slice x160 -> x7, local copies, waits for them, and re-layouts: 98.5 us -> 6.99 us  [the longest x2 3.01 us: halve_rows(): away = lax.dynamic_slice_in_dim(array[0], (1 - spot) * half, half, 0)]
  transfers between devices with their start and end apart: 46 -> 28, of which waited for: 13 -> 6; matrix products, arithmetic and copies ran while one was open for 67% -> 15% of each run, Pallas kernels for 0% -> 65%
where the time goes in v1:
time: 929 us; the launch traced here: 920 us
  Pallas kernels  674 us (73%)
  local copies, waits for them, and re-layouts  81.4 us (9%)
  waiting for transfers between devices  54.8 us (6%)
  other arithmetic  40.8 us (4%)
  matrix products  30.4 us (3%)
  starting transfers between devices  22.8 us (2%)
  between operations  15.3 us (2%)
    pallas_call x3, Pallas kernels, attend_backward(): pl.pallas_call(functools.partial(backward_kernel, causal, aligned, chunk_...  254 us
    pallas_call x9, Pallas kernels, rows_call(): pl.pallas_call(kernel, grid=(rows // step,), in_specs=in_specs, out_specs...  187 us
    pallas_call x3, Pallas kernels, attend_forward(): pl.pallas_call(functools.partial(forward_kernel, causal, aligned), grid=(...  136 us
    pallas_call x11, Pallas kernels, fill_call(): pl.pallas_call(kernel, grid=grid, in_specs=in_specs, out_specs=out_spec,...  96.7 us
    all_gather x4, waiting for transfers between devices, gather(): return lax.all_gather(whole, 'wide', axis=0, tiled=True)  40.1 us
    dot_general x5, matrix products, matmul(): return jnp.dot(left_side, right_side, preferred_element_type=F32)  30.4 us
  transfers between devices with their start and end apart: 28, of which 6 were waited for; matrix products, arithmetic and copies ran while one was open for 15% of the time, Pallas kernels for 65%

profile of v1, /device:TPU:0, one launch (start us, length us, event | category | flops | bytes accessed | tf_op | source)
XLA Modules:
  0.0 919.5 jit_solution(10331972374228376582)
XLA Ops:
  27.4 34.8 %all-gather.5.cloned.1.call-done.refs_1_ = bf16[768,2432]{1,0:T(8,128)(2,1)} async-done(((bf16[48,2432]{1,0:T(8,128)(2,1)}), bf16[768,2432]{1,0:T(8,128)(2,1)}) %all-gather.5.cloned.1.call-update) | async-done | bytes 3735568 | tf_op jit(solution)/shard_map/all_gather | solution.py:891
  78.0 9.6 %fusion.query_ref.key_ref.value_ref = bf16[1,2048,2304]{2,1,0:T(8,128)(2,1)} fusion(bf16[2048,768]{1,0:T(8,128)(2,1)S(1)} %multiply_convert_fusion.rows_ref, bf16[768,2432]{1,0:T(8,128)(2,1)S(1)} %copy-done.10), kind=kOutput, calls=%fused_computation.1 | convolution fusion | flops 7252475904 | bytes 16121856 | tf_op jit(solution)/shard_map/dot_general | solution.py:38
  87.9 71.6 %attend_forward.3 = (bf16[1,2048,768]{2,1,0:T(8,128)(2,1)}, f32[1,2048,768]{2,1,0:T(8,128)}, f32[1,2048,768]{2,1,0:T(8,128)}) custom-call(s32[2]{0:T(128)} %pad_add_fusion.1.scalars_ref, bf16[1,2048,2304]{2,1,0:T(8,128)(2,1)} %fusion.query_ref.key_ref.value_ref, bf16[1,2048,2304]{2,1,0:T(8,128)(2,1)} %fusion.query_ref.key_ref.value_ref, ...), custom_call_target="tpu_custom_call" | custom-call | flops 1000 | bytes 1000 | tf_op jit(solution)/shard_map/attend_forward/pallas_call | solution.py:734
  159.5 4.8 turn_rows.1.left_ref
  174.2 44.3 %layer_forward.2 = (f32[2048,768]{1,0:T(8,128)}, bf16[768,2048]{1,0:T(8,128)(2,1)}, bf16[2048,4096]{1,0:T(8,128)(2,1)}, bf16[2048,2048]{1,0:T(8,128)(2,1)}, bf16...) custom-call(bf16[2048,768]{1,0:T(8,128)(2,1)} %bitcast.139, ...), custom_call_target="tpu_custom_call" | custom-call | flops 1000 | bytes 1000 | tf_op jit(solution)/shard_map/layer_forward/pallas_call | solution.py:550
  224.8 7.7 fusion.2.query_ref.key_ref.value_ref
  234.0 23.7 %attend_forward.4 = (bf16[1,1024,768]{2,1,0:T(8,128)(2,1)}, f32[1,1024,768]{2,1,0:T(8,128)}, f32[1,1024,768]{2,1,0:T(8,128)}) custom-call(s32[2]{0:T(128)} %pad_add_fusion.scalars_ref, bf16[1,1024,2304]{2,1,0:T(8,128)(2,1)} %fusion.2.query_ref.key_ref.value_ref, bf16[1,1024,2304]{2,1,0:T(8,128)(2,1)} %fusion.2.query_ref.key_ref.value_ref, ...), custom_call_target="tpu_custom_call" | custom-call | flops 1000 | bytes 1000 | tf_op jit(solution)/shard_map/attend_forward/pallas_call | solution.py:734
  264.2 7.1 fusion.1.key_ref.value_ref
  273.8 40.2 %attend_forward.5 = (bf16[1,1024,768]{2,1,0:T(8,128)(2,1)}, f32[1,1024,768]{2,1,0:T(8,128)}, f32[1,1024,768]{2,1,0:T(8,128)}) custom-call(s32[2]{0:T(128)} %pad_add_fusion.1.scalars_ref, bf16[1,1024,768]{2,1,0:T(8,128)(2,1)} %fusion.9.query_ref, bf16[1,2048,1536]{2,1,0:T(8,128)(2,1)} %fusion.1.key_ref.value_ref, bf16[1,2048,1536]{2,1,0:T(8,128)(2,1)} %fusion.1.key_ref.value_ref), custom_call_target="tpu_custom_call" | custom-call | flops 1000 | bytes 1000 | tf_op jit(solution)/shard_map/attend_forward/pallas_call | solution.py:734
  314.1 4.4 all-gather.11.cloned.1.call-done.gate_up_ref.packed_ref.output_ref
  318.5 25.2 %layer_forward.3 = (f32[1024,768]{1,0:T(8,128)}, bf16[768,1024]{1,0:T(8,128)(2,1)}, bf16[1024,4096]{1,0:T(8,128)(2,1)}, bf16[2048,1024]{1,0:T(8,128)(2,1)}, bf16[1024,768]{1,0:T(8,128)(2,1)}) custom-call(bf16[1024,768]{1,0:T(8,128)(2,1)} %bitcast.142, f32[1024,768]{1,0:T(8,128)} %copy-done.1, ...), custom_call_target="tpu_custom_call" | custom-call | flops 1000 | bytes 1000 | tf_op jit(solution)/shard_map/layer_forward/pallas_call | solution.py:550
  343.8 24.0 %layer_backward.2 = (bf16[1024,4096]{1,0:T(8,128)(2,1)}, f32[1024,768]{1,0:T(8,128)}, bf16[1024,768]{1,0:T(8,128)(2,1)}, bf16[1024,768]{1,0:T(8,128)(2,1)}, f32[8,768]{1,0:T(8,128)}) custom-call(bf16[1024,768]{1,0:T(8,128)(2,1)} %bitcast.135, bf16[1024,4096]{1,0:T(8,128)(2,1)} %get-tuple-element.139.slopes_ref, f32[1024,768]{1,0:T(8,128)} %get-tuple-element.140.middle_ref, ...), custom_call_target="tpu_custom_call" | custom-call | flops 1000 | bytes 1000 | tf_op jit(solution)/shard_map/layer_backward/pallas_call | solution.py:550
  367.8 11.0 %weight_grad.9.refs_0_ = bf16[768,6144]{1,0:T(8,128)(2,1)} custom-call(bf16[768,1024]{1,0:T(8,128)(2,1)} %get-tuple-element.138.left_ref, bf16[1024,4096]{1,0:T(8,128)(2,1)} %get-tuple-element.141.right_ref), custom_call_target="tpu_custom_call" | custom-call | flops 1000 | bytes 1000 | tf_op jit(solution)/shard_map/weight_grad/pallas_call | solution.py:665
  378.7 7.2 down_grad.2
  390.4 76.2 %attend_backward.3 = (bf16[1,1024,768]{2,1,0:T(8,128)(2,1)}, bf16[1,2048,1536]{2,1,0:T(8,128)(2,1)}) custom-call(s32[2]{0:T(128)} %pad_add_fusion.1.scalars_ref, bf16[1,1024,768]{2,1,0:T(8,128)(2,1)} %fusion.9.query_ref, bf16[1,2048,1536]{2,1,0:T(8,128)(2,1)} %fusion.1.key_ref.value_ref, bf16[1,2048,1536]{2,1,0:T(8,128)(2,1)} %fusion.1.key_ref.value_ref, ...), custom_call_target="tpu_custom_call" | custom-call | flops 1000 | bytes 1000 | tf_op jit(solution)/shard_map/attend_backward/pallas_call | solution.py:796
  466.6 4.4 weight_grad.11.refs_0_
  471.0 9.6 %weight_grad.12 = bf16[768,3072]{1,0:T(8,128)(2,1)} custom-call(bf16[768,2048]{1,0:T(8,128)(2,1)} %get-tuple-element.131.left_ref, bf16[2048,1536]{1,0:T(8,128)(2,1)} %bitcast.133, bf16[768,3072]{1,0:T(8,128)(2,1)} %weight_grad.11.refs_0_), custom_call_target="tpu_custom_call", output_to_operand_aliasing={{}: (2, {})} | custom-call | flops 1000 | bytes 1000 | tf_op jit(solution)/shard_map/weight_grad/pallas_call | solution.py:665
  484.0 9.9 %project_back.4 = (f32[1024,768]{1,0:T(8,128)}, f32[8,768]{1,0:T(8,128)}, bf16[1024,768]{1,0:T(8,128)(2,1)}, bf16[1024,768]{1,0:T(8,128)(2,1)}) custom-call(bf16[1024,768]{1,0:T(8,128)(2,1)} %bitcast.145, bf16[768,3072]{1,0:T(8,128)(2,1)} %all-gather.9.cloned.1.call-done.refs_1_.refs_5_, f32[1024,768]{1,0:T(8,128)} %get-tuple-element.151.refs_2_, ...), custom_call_target="tpu_custom_call" | custom-call | flops 1000 | bytes 1000 | tf_op jit(solution)/shard_map/project_back/pallas_call | solution.py:550
  493.9 4.4 weight_grad.13.refs_0_
  498.3 36.9 %attend_backward.4 = bf16[1,1024,2304]{2,1,0:T(8,128)(2,1)} custom-call(s32[2]{0:T(128)} %pad_add_fusion.scalars_ref, bf16[1,1024,2304]{2,1,0:T(8,128)(2,1)} %fusion.2.query_ref.key_ref.value_ref, bf16[1,1024,2304]{2,1,0:T(8,128)(2,1)} %fusion.2.query_ref.key_ref.value_ref, bf16[1,1024,2304]{2,1,0:T(8,128)(2,1)} %fusion.2.query_ref.key_ref.value_ref, ...), custom_call_target="tpu_custom_call" | custom-call | flops 1000 | bytes 1000 | tf_op jit(solution)/shard_map/attend_backward/pallas_call | solution.py:796
  535.2 8.1 weight_grad.14
  543.4 13.8 %project_back.6 = (f32[2048,768]{1,0:T(8,128)}, f32[8,768]{1,0:T(8,128)}, bf16[2048,768]{1,0:T(8,128)(2,1)}) custom-call(bf16[2048,1536]{1,0:T(8,128)(2,1)} %bitcast.134, bf16[768,3072]{1,0:T(8,128)(2,1)} %all-gather.9.cloned.1.call-done.refs_1_.refs_5_, bf16[2048,768]{1,0:T(8,128)(2,1)} %bitcast.141, f32[2048,768]{1,0:T(8,128)} %get-tuple-element.169.refs_3_, ...), custom_call_target="tpu_custom_call" | custom-call | flops 1000 | bytes 1000 | tf_op jit(solution)/shard_map/project_back/pallas_call | solution.py:550
  557.2 39.3 %layer_backward.3 = (bf16[2048,4096]{1,0:T(8,128)(2,1)}, f32[2048,768]{1,0:T(8,128)}, bf16[2048,768]{1,0:T(8,128)(2,1)}, bf16[2048,768]{1,0:T(8,128)(2,1)}, f32[8,768]{1,0:T(8,128)}) custom-call(f32[2048,768]{1,0:T(8,128)} %get-tuple-element.172.grad_ref, bf16[2048,4096]{1,0:T(8,128)(2,1)} %get-tuple-element.173.slopes_ref, ...), custom_call_target="tpu_custom_call" | custom-call | flops 1000 | bytes 1000 | tf_op jit(solution)/shard_map/layer_backward/pallas_call | solution.py:550
  596.5 18.3 %weight_grad.15.refs_0_ = bf16[768,6144]{1,0:T(8,128)(2,1)} custom-call(bf16[768,2048]{1,0:T(8,128)(2,1)} %get-tuple-element.171.left_ref, bf16[2048,4096]{1,0:T(8,128)(2,1)} %get-tuple-element.175.right_ref), custom_call_target="tpu_custom_call" | custom-call | flops 1000 | bytes 1000 | tf_op jit(solution)/shard_map/weight_grad/pallas_call | solution.py:665
  614.8 10.8 %down_grad.3 = bf16[768,6144]{1,0:T(8,128)(2,1)} custom-call(bf16[2048,2048]{1,0:T(8,128)(2,1)} %get-tuple-element.166.hidden_ref, bf16[2048,768]{1,0:T(8,128)(2,1)} %get-tuple-element.170.right_ref, bf16[768,6144]{1,0:T(8,128)(2,1)} %weight_grad.15.refs_0_), custom_call_target="tpu_custom_call", output_to_operand_aliasing={{}: (2, {})} | custom-call | flops 1000 | bytes 1000 | tf_op jit(solution)/shard_map/down_grad/pallas_call | solution.py:665
  627.5 10.1 %project_back.5 = (f32[1024,768]{1,0:T(8,128)}, f32[8,768]{1,0:T(8,128)}) custom-call(bf16[1024,2304]{1,0:T(8,128)(2,1)} %bitcast.131, bf16[768,9216]{1,0:T(8,128)(2,1)} %all-gather.7.cloned.1.call-done.gate_up_ref.packed_ref.output_ref.refs_1_, f32[1024,768]{1,0:T(8,128)} %get-tuple-element.162.refs_2_, bf16[1024,768]{1,0:T(8,128)(2,1)} %bitcast.132, ...), custom_call_target="tpu_custom_call" | custom-call | flops 1000 | bytes 1000 | tf_op jit(solution)/shard_map/project_back/pallas_call | solution.py:550
  641.3 6.6 weight_grad.16.refs_0_
  647.9 141.2 %attend_backward.5 = bf16[1,2048,2304]{2,1,0:T(8,128)(2,1)} custom-call(s32[2]{0:T(128)} %pad_add_fusion.1.scalars_ref, bf16[1,2048,2304]{2,1,0:T(8,128)(2,1)} %fusion.query_ref.key_ref.value_ref, bf16[1,2048,2304]{2,1,0:T(8,128)(2,1)} %fusion.query_ref.key_ref.value_ref, bf16[1,2048,2304]{2,1,0:T(8,128)(2,1)} %fusion.query_ref.key_ref.value_ref, ...), custom_call_target="tpu_custom_call" | custom-call | flops 1000 | bytes 1000 | tf_op jit(solution)/shard_map/attend_backward/pallas_call | solution.py:796
  791.7 12.1 %weight_grad.17 = bf16[768,3072]{1,0:T(8,128)(2,1)} custom-call(bf16[768,2048]{1,0:T(8,128)(2,1)} %turn_rows.1.left_ref, bf16[2048,2304]{1,0:T(8,128)(2,1)} %bitcast.126, bf16[768,3072]{1,0:T(8,128)(2,1)} %weight_grad.16.refs_0_), custom_call_target="tpu_custom_call", output_to_operand_aliasing={{}: (2, {})} | custom-call | flops 1000 | bytes 1000 | tf_op jit(solution)/shard_map/weight_grad/pallas_call | solution.py:665
  834.5 16.0 %project_back.7 = (f32[2048,768]{1,0:T(8,128)}, f32[8,768]{1,0:T(8,128)}) custom-call(bf16[2048,2304]{1,0:T(8,128)(2,1)} %bitcast.127, bf16[768,2432]{1,0:T(8,128)(2,1)} %all-gather.5.cloned.1.call-done.refs_1_, f32[2048,768]{1,0:T(8,128)} %get-tuple-element.194.refs_2_, f32[2048,768]{1,0:T(8,128)} %copy-done, f32[8,768]{1,0:T(8,128)} %copy-done.17), custom_call_target="tpu_custom_call" | custom-call | flops 1000 | bytes 1000 | tf_op jit(solution)/shard_map/project_back/pallas_call | solution.py:550
  886.7 9.8 %collective-permute-done.11 = bf16[1024,768]{1,0:T(8,128)(2,1)} collective-permute-done((bf16[1024,768]{1,0:T(8,128)(2,1)}, bf16[1024,768]{1,0:T(8,128)(2,1)}, u32[]{:S(2)}, u32[]{:S(2)}) %collective-permute-start.11) | collective-permute-done | bytes 1572896 | tf_op jit(solution)/shard_map/ppermute | solution.py:859
  901.8 5.1 broadcast_select_fusion
  (306 shorter events, 156.0 us)
Async XLA Ops:
  7.2 55.0 %all-gather.5.cloned.1.call-start = ((), (), s32[]{:S(2)}) async-start(), calls=%async_computation.5 | async-start | bytes 3969024 | tf_op jit(solution)/shard_map/all_gather | solution.py:891
  11.2 163.0 %all-gather.7.cloned.1.call-start = ((), (), s32[]{:S(2)}) async-start(), calls=%async_computation.6 | async-start | bytes 15040512 | tf_op jit(solution)/shard_map/all_gather | solution.py:891
  14.9 242.9 %all-gather.9.cloned.1.call-start = ((), (), s32[]{:S(2)}) async-start(), calls=%async_computation.7 | async-start | bytes 5013504 | tf_op jit(solution)/shard_map/all_gather | solution.py:891
  16.1 302.5 %all-gather.11.cloned.1.call-start = ((), (), s32[]{:S(2)}) async-start(), calls=%async_computation.8 | async-start | bytes 11280384 | tf_op jit(solution)/shard_map/all_gather | solution.py:891
  19.5 43.8 %collective-permute-start = (bf16[1024,768]{1,0:T(8,128)(2,1)}, bf16[1024,768]{1,0:T(8,128)(2,1)S(1)}, u32[]{:S(2)}, u32[]{:S(2)}) collective-permute-start(bf16[1024,768]{1,0:T(8,128)(2,1)} %get-tuple-element.287), channel_id=1, source_target_pairs={{0,1},{1,0},{2,3},{3,2},{4,5},{5,4},{6,7},{7,6},{8,9},{9,8},{10,11... | collective-permute-start | bytes 4718600 | tf_op jit(solution)/shard_map/ppermute | solution.py:859
  22.4 45.0 %copy-start.41 = (pred[2]{0:T(512)(128)(4,1)}, pred[2]{0:T(512)(128)(4,1)S(1)}, u32[]{:S(2)}) copy-start(pred[2]{0:T(512)(128)(4,1)S(1)} %iota_compare_fusion.2) | copy-start | bytes 10
  68.7 95.6 %collective-permute-start.3 = (bf16[512,768]{1,0:T(8,128)(2,1)}, bf16[512,768]{1,0:T(8,128)(2,1)}, u32[]{:S(2)}, u32[]{:S(2)}) collective-permute-start(bf16[512,768]{1,0:T(8,128)(2,1)} %get-tuple-element.291), channel_id=1, source_target_pairs={{0,1},{1,0},{2,3},{3,2},{4,5},{5,4},{6,7},{7,6},{8,9},{9,8},{10,11... | collective-permute-start | bytes 2359304 | tf_op jit(solution)/shard_map/ppermute | solution.py:859
  71.5 92.8 %collective-permute-start.1 = (bf16[512,768]{1,0:T(8,128)(2,1)}, bf16[512,768]{1,0:T(8,128)(2,1)}, u32[]{:S(2)}, u32[]{:S(2)}) collective-permute-start(bf16[512,768]{1,0:T(8,128)(2,1)} %get-tuple-element.293), channel_id=1, source_target_pairs={{0,1},{1,0},{2,3},{3,2},{4,5},{5,4},{6,7},{7,6},{8,9},{9,8},{10,11... | collective-permute-start | bytes 2359304 | tf_op jit(solution)/shard_map/ppermute | solution.py:859
  73.9 94.8 %collective-permute-start.2 = (bf16[1024,768]{1,0:T(8,128)(2,1)}, bf16[1024,768]{1,0:T(8,128)(2,1)}, u32[]{:S(2)}, u32[]{:S(2)}) collective-permute-start(bf16[1024,768]{1,0:T(8,128)(2,1)} %get-tuple-element.285), channel_id=1, source_target_pairs={{0,1},{1,0},{2,3},{3,2},{4,5},{5,4},{6,7},{7,6},{8,9},{9,8},{10,11... | collective-permute-start | bytes 4718600 | tf_op jit(solution)/shard_map/ppermute | solution.py:859
  168.7 89.1 %copy-start.2 = (bf16[1,1024,768]{2,1,0:T(8,128)(2,1)}, bf16[1,1024,768]{2,1,0:T(8,128)(2,1)S(1)}, u32[]{:S(2)}) copy-start(bf16[1,1024,768]{2,1,0:T(8,128)(2,1)S(1)} %get-tuple-element.124) | copy-start | bytes 4718596
  174.2 44.6 %copy-start.38 = (bf16[48,768]{1,0:T(8,128)(2,1)S(1)}, bf16[48,768]{1,0:T(8,128)(2,1)}, u32[]{:S(2)}) copy-start(bf16[48,768]{1,0:T(8,128)(2,1)} %param.35) | copy-start | bytes 221188
  219.8 323.6 %reduce-scatter.6.cloned.1.call-start = ((), (), s32[]{:S(2)}) async-start(), calls=%async_computation.9 | async-start | bytes 10027008 | tf_op jit(solution)/shard_map/reduce_scatter | solution.py:894
  232.6 81.6 %collective-permute-start.4 = (bf16[1024,768]{1,0:T(8,128)(2,1)}, bf16[1024,768]{1,0:T(8,128)(2,1)S(1)}, u32[]{:S(2)}, u32[]{:S(2)}) collective-permute-start(bf16[1024,768]{1,0:T(8,128)(2,1)} %get-tuple-element.282), channel_id=1, source_target_pairs={{0,1},{1,0},{2,3},{3,2},{4,5},{5,4},{6,7},{7,6},{8,9},{9,8},{10,11... | collective-permute-start | bytes 4718600 | tf_op jit(solution)/shard_map/ppermute | solution.py:859
  385.9 239.6 %reduce-scatter.10.cloned.1.call-start = ((), (), s32[]{:S(2)}) async-start(), calls=%async_computation.11 | async-start | bytes 5013504 | tf_op jit(solution)/shard_map/reduce_scatter | solution.py:894
  480.6 311.1 %reduce-scatter.8.cloned.1.call-start = ((), (), s32[]{:S(2)}) async-start(), calls=%async_computation.10 | async-start | bytes 5013504 | tf_op jit(solution)/shard_map/reduce_scatter | solution.py:894
  483.0 60.4 %collective-permute-start.5 = (bf16[512,768]{1,0:T(8,128)(2,1)S(1)}, bf16[512,768]{1,0:T(8,128)(2,1)S(1)}, u32[]{:S(2)}, u32[]{:S(2)}) collective-permute-start(bf16[512,768]{1,0:T(8,128)(2,1)S(1)} %get-tuple-element.288), channel_id=1, source_target_pairs={{0,1},{1,0},{2,3},{3,2},{4,5},{5,4},{6,7},{7,6},{8,9},{9,8},{10,11... | collective-permute-start | bytes 2359304 | tf_op jit(solution)/shard_map/ppermute | solution.py:859
  543.4 248.3 %reduce-scatter.12.cloned.1.call-start = ((), (), s32[]{:S(2)}) async-start(), calls=%async_computation.12 | async-start | bytes 10027008 | tf_op jit(solution)/shard_map/reduce_scatter | solution.py:894
  625.6 274.2 %reduce-scatter.14.cloned.1.call-start = ((), (), s32[]{:S(2)}) async-start(), calls=%async_computation.13 | async-start | bytes 5013504 | tf_op jit(solution)/shard_map/reduce_scatter | solution.py:894
  626.5 162.8 %collective-permute-start.8 = (bf16[48,3072]{1,0:T(8,128)(2,1)S(1)}, bf16[48,3072]{1,0:T(8,128)(2,1)S(1)}, u32[]{:S(2)}, u32[]{:S(2)}) collective-permute-start(bf16[48,3072]{1,0:T(8,128)(2,1)S(1)} %copy-done.33), channel_id=1, source_target_pairs={{0,1},{1,0},{2,3},{3,2},{4,5},{5,4},{6,7},{7,6},{8,9},{9,8},{10,11... | collective-permute-start | bytes 884744 | tf_op jit(solution)/shard_map/ppermute | solution.py:859
  639.3 152.5 %collective-permute-start.6 = (bf16[512,768]{1,0:T(8,128)(2,1)S(1)}, bf16[512,768]{1,0:T(8,128)(2,1)}, u32[]{:S(2)}, u32[]{:S(2)}) collective-permute-start(bf16[512,768]{1,0:T(8,128)(2,1)S(1)} %dynamic-slice_convert_fusion.1), channel_id=1, source_target_pairs={{0,1},{1,0},{2,3},{3,2},{4,5},{5,4},{6,7},{7,6},{8,9},{9,8},{10,11... | collective-permute-start | bytes 2359304 | tf_op jit(solution)/shard_map/ppermute | solution.py:859
  640.2 150.1 %collective-permute-start.7 = (bf16[48,6144]{1,0:T(8,128)(2,1)S(1)}, bf16[48,6144]{1,0:T(8,128)(2,1)S(1)}, u32[]{:S(2)}, u32[]{:S(2)}) collective-permute-start(bf16[48,6144]{1,0:T(8,128)(2,1)S(1)} %copy-done.30), channel_id=1, source_target_pairs={{0,1},{1,0},{2,3},{3,2},{4,5},{5,4},{6,7},{7,6},{8,9},{9,8},{10,11... | collective-permute-start | bytes 1769480 | tf_op jit(solution)/shard_map/ppermute | solution.py:859
  647.9 141.3 %copy-start.18 = (f32[1024,768]{1,0:T(8,128)S(1)}, f32[1024,768]{1,0:T(8,128)}, u32[]{:S(2)}) copy-start(f32[1024,768]{1,0:T(8,128)} %get-tuple-element.163) | copy-start | bytes 9437188
  813.7 18.3 %collective-permute-start.9 = (bf16[48,3072]{1,0:T(8,128)(2,1)}, bf16[48,3072]{1,0:T(8,128)(2,1)}, u32[]{:S(2)}, u32[]{:S(2)}) collective-permute-start(bf16[48,3072]{1,0:T(8,128)(2,1)} %reduce-scatter.8.cloned.1.call-done), channel_id=1, source_target_pairs={{0,1},{1,0},{2,3},{3,2},{4,5},{5,4},{6,7},{7,6},{8,9},{9,8},{10,11... | collective-permute-start | bytes 884744 | tf_op jit(solution)/shard_map/ppermute | solution.py:859
  814.6 19.9 %collective-permute-start.10 = (bf16[48,6144]{1,0:T(8,128)(2,1)}, bf16[48,6144]{1,0:T(8,128)(2,1)}, u32[]{:S(2)}, u32[]{:S(2)}) collective-permute-start(bf16[48,6144]{1,0:T(8,128)(2,1)} %reduce-scatter.12.cloned.1.call-done), channel_id=1, source_target_pairs={{0,1},{1,0},{2,3},{3,2},{4,5},{5,4},{6,7},{7,6},{8,9},{9,8},{10,11... | collective-permute-start | bytes 1769480 | tf_op jit(solution)/shard_map/ppermute | solution.py:859
  858.0 5.8 collective-permute-start.14
  858.0 5.8 collective-permute-start.13
  858.1 5.7 collective-permute-start.12
  859.9 36.6 %collective-permute-start.11 = (bf16[1024,768]{1,0:T(8,128)(2,1)}, bf16[1024,768]{1,0:T(8,128)(2,1)}, u32[]{:S(2)}, u32[]{:S(2)}) collective-permute-start(bf16[1024,768]{1,0:T(8,128)(2,1)} %dynamic-slice_convert_fusion), channel_id=1, source_target_pairs={{0,1},{1,0},{2,3},{3,2},{4,5},{5,4},{6,7},{7,6},{8,9},{9,8},{10,11... | collective-permute-start | bytes 4718600 | tf_op jit(solution)/shard_map/ppermute | solution.py:859
  864.4 21.3 %collective-permute-start.17 = (f32[8,768]{1,0:T(8,128)}, f32[8,768]{1,0:T(8,128)}, u32[]{:S(2)}, u32[]{:S(2)}) collective-permute-start(f32[8,768]{1,0:T(8,128)} %add_add_fusion), channel_id=1, source_target_pairs={{0,24},{2,26},{4,28},{6,30},{8,16},{10,18},{12,20},{14,22},{16,8},... | collective-permute-start | bytes 73736 | tf_op jit(solution)/shard_map/ppermute | solution.py:901
  866.4 19.3 %collective-permute-start.16 = (f32[8,768]{1,0:T(8,128)}, f32[8,768]{1,0:T(8,128)}, u32[]{:S(2)}, u32[]{:S(2)}) collective-permute-start(f32[8,768]{1,0:T(8,128)} %add_add_fusion), channel_id=1, source_target_pairs={{0,16},{2,18},{4,20},{6,22},{8,24},{10,26},{12,28},{14,30},{16,0},... | collective-permute-start | bytes 73736 | tf_op jit(solution)/shard_map/ppermute | solution.py:901
  866.4 19.3 %collective-permute-start.15 = (f32[8,768]{1,0:T(8,128)}, f32[8,768]{1,0:T(8,128)}, u32[]{:S(2)}, u32[]{:S(2)}) collective-permute-start(f32[8,768]{1,0:T(8,128)} %add_add_fusion), channel_id=1, source_target_pairs={{0,8},{2,10},{4,12},{6,14},{8,0},{10,2},{12,4},{14,6},{16,24},{18,... | collective-permute-start | bytes 73736 | tf_op jit(solution)/shard_map/ppermute | solution.py:901
  900.8 8.4 collective-permute-start.18
  (53 other events, 360.5 us)
Sparse Core Ops, SparseCore 0:
  11.4 50.7 all-gather.4
  64.5 109.7 all-gather.6
  177.1 51.4 all-gather.8
  231.3 87.2 all-gather.10
  386.0 109.5 reduce-scatter.5
  499.8 75.2 reduce-scatter.9
  579.0 74.6 reduce-scatter.7
  658.3 110.4 reduce-scatter.11
  804.0 74.0 reduce-scatter.13

commit v2 on v1

--- a/solution.py
+++ b/solution.py
@@ -824,6 +824,40 @@
     )(scalars, query_array, key_array, value_array, head_grad, exact, total)
 
 
+def place_kernel(spot_ref, own_ref, got_ref, out_ref):
+    slot = pl.program_id(1)
+
+    @pl.when(slot == spot_ref[0])
+    def keep():
+        out_ref[0] = own_ref[...]
+
+    @pl.when(slot != spot_ref[0])
+    def take():
+        out_ref[0] = got_ref[...].astype(out_ref.dtype)
+
+
+def place_halves(spot, array, got):
+    half = got.shape[0]
+    step = min(512, half)
+    blocks = half // step
+    return pl.pallas_call(
+        place_kernel,
+        grid_spec=pltpu.PrefetchScalarGridSpec(
+            num_scalar_prefetch=1,
+            grid=(blocks, 2),
+            in_specs=[
+                pl.BlockSpec((step, D), lambda m, i, spot_ref: (spot_ref[0] * blocks + m, 0)),
+                pl.BlockSpec((step, D), lambda m, i, spot_ref: (m, 0)),
+            ],
+            out_specs=pl.BlockSpec((1, step, D), lambda m, i, spot_ref: (i, m, 0)),
+        ),
+        out_shape=jax.ShapeDtypeStruct((2, half, D), array.dtype),
+        compiler_params=pltpu.CompilerParams(vmem_limit_bytes=VMEM_BYTES),
+        cost_estimate=pl.CostEstimate(flops=1000, bytes_accessed=24000000, transcendentals=0),
+        name="place_halves",
+    )(spot.astype(jnp.int32).reshape(1), array, got)
+
+
 def in_order(first, second):
     return lax.optimization_barrier((first, second))
 
@@ -1163,24 +1197,24 @@
         patch_grad, enc_slopes, patch_middle, second_group, gains, 1
     )
     enc_head_grad = enc_head_grad.reshape(items, patch_rows, D)
-    third_width = 2 * FF + FF
+    third_width = 2 * FF + FF + D
     third_terms = fill_weight_grad(None, third_width, 0, mlp_input, enc_gate_grad, True)
     third_terms = fill_down_grad(
         third_terms, third_width, 2 * FF, shard_rows, enc_hidden, down_grad
     )
-    (third_terms, second_sum), (enc_out_grad, enc_head_grad) = in_order(
-        (third_terms, second_sum), (enc_out_grad, enc_head_grad)
+    third_terms = fill_weight_grad(
+        third_terms, third_width, 3 * FF, enc_attended_flat, enc_out_grad
+    )
+    (third_terms, second_sum), enc_head_grad = in_order(
+        (third_terms, second_sum), enc_head_grad
     )
     third_sum = scatter(third_terms)
-    fourth_width = D + 3 * D
-    fourth_terms = fill_weight_grad(None, fourth_width, 0, enc_attended_flat, enc_out_grad)
     grad_dec_gate_up, grad_dec_down = finish(first_sum, (2 * FF, FF))
     grad_cross_output, grad_cross_query, grad_memory_kv = finish(second_sum, (D, D, 2 * D))
     text_back, gain_self = project_back(
         [(self_qkv_grad, second_group, self_project_at)], middle_grad, text_start, gains, 2
     )
     text_back_sent, unused = send_rows(text_back.reshape(items, text_rows, D))
-    fourth_terms, enc_head_grad = in_order(fourth_terms, enc_head_grad)
 
     enc_qkv_grad = joined(
         attend_backward(
@@ -1211,16 +1245,18 @@
         grad_memory_kv,
     ) = late
     fourth_terms = fill_weight_grad(
-        fourth_terms, fourth_width, D, attn_turned, enc_qkv_grad, True
+        None, 3 * D, 0, attn_turned, enc_qkv_grad, True
     )
     fourth_terms, enc_qkv_grad = in_order(fourth_terms, enc_qkv_grad)
     fourth_sum = scatter(fourth_terms)
     self_got, third_got = exchange(self_sum), exchange(third_sum)
-    (self_got, third_got), enc_qkv_grad = in_order((self_got, third_got), enc_qkv_grad)
 
     start_grad, gain_attn = project_back(
         [(enc_qkv_grad, first_group, (3 * D, 0))], enc_middle_grad, patch_start, gains, 0
     )
+    floating = (self_got, third_got, patch_sent, text_sent, text_back_sent)
+    floating, start_grad = in_order(floating, start_grad)
+    self_got, third_got, patch_sent, text_sent, text_back_sent = floating
     patch_back_sent, start_grad = send_rows(
         start_grad.reshape(items, patch_rows, D), start_grad
     )
@@ -1230,17 +1266,20 @@
     small_own = lax.dynamic_slice_in_dim(
         sum_small(small_term), lax.axis_index("wide") * shard_rows, shard_rows, 1
     ).T
-    small_own = jnp.pad(small_own.astype(BF16), ((0, 0), (0, PAIR - small_own.shape[1])))
+    (grad_small,) = finish(small_own.astype(BF16), (small_own.shape[1],))
 
     grad_self_output, grad_self_project = finish(self_sum, (D, 3 * D), self_got)
-    grad_enc_gate_up, grad_enc_down = finish(third_sum, (2 * FF, FF), third_got)
-    grad_enc_output, grad_enc_project, grad_small = finish(
-        jnp.concatenate([fourth_sum, small_own], axis=1), (D, 3 * D, PAIR)
-    )
+    grad_enc_gate_up, grad_enc_down, grad_enc_output = finish(
+        third_sum, (2 * FF, FF, D), third_got
+    )
+    (grad_enc_project,) = finish(fourth_sum, (3 * D,))
     patch_output = place_rows(patch_sent)
     text_output = place_rows(text_sent)
     text_input_grad = place_rows(text_back_sent)
-    patch_input_grad = place_rows(patch_back_sent)
+    if swapped:
+        patch_input_grad = place_halves(spot, start_grad, patch_back_sent[1])
+    else:
+        patch_input_grad = patch_back_sent[0]
     grad_cross_project = jnp.concatenate([grad_cross_query, by_side(grad_memory_kv)], axis=1)
     return (
         patch_output,

time: 929 us -> 901 us (0.970)
  local copies, waits for them, and re-layouts: 81.4 us -> 57.9 us
  other arithmetic: 40.8 us -> 25.6 us
  transfers between devices with their start and end apart: 28 -> 29, of which waited for: 6 -> 5; matrix products, arithmetic and copies ran while one was open for 15% -> 11% of each run, Pallas kernels for 65% -> 67%
where the time goes in v2:
time: 901 us; the launch traced here: 893 us
  Pallas kernels  681 us (76%)
  waiting for transfers between devices  58.6 us (7%)
  local copies, waits for them, and re-layouts  57.9 us (6%)
  matrix products  30.3 us (3%)
  other arithmetic  25.6 us (3%)
  starting transfers between devices  23.7 us (3%)
  between operations  15.3 us (2%)
    pallas_call x3, Pallas kernels, attend_backward(): pl.pallas_call(functools.partial(backward_kernel, causal, aligned, chunk_...  254 us
    pallas_call x9, Pallas kernels, rows_call(): pl.pallas_call(kernel, grid=(rows // step,), in_specs=in_specs, out_specs...  188 us
    pallas_call x3, Pallas kernels, attend_forward(): pl.pallas_call(functools.partial(forward_kernel, causal, aligned), grid=(...  136 us
    pallas_call x11, Pallas kernels, fill_call(): pl.pallas_call(kernel, grid=grid, in_specs=in_specs, out_specs=out_spec,...  96.9 us
    all_gather x4, waiting for transfers between devices, gather(): return lax.all_gather(whole, 'wide', axis=0, tiled=True)  43.1 us
    dot_general x5, matrix products, matmul(): return jnp.dot(left_side, right_side, preferred_element_type=F32)  30.3 us
  transfers between devices with their start and end apart: 29, of which 5 were waited for; matrix products, arithmetic and copies ran while one was open for 11% of the time, Pallas kernels for 67%

profile of v2, /device:TPU:0, one launch (start us, length us, event | category | flops | bytes accessed | tf_op | source)
XLA Modules:
  0.0 892.5 jit_solution(2589897428383489576)
XLA Ops:
  26.9 35.1 %all-gather.5.cloned.1.call-done.refs_1_ = bf16[768,2432]{1,0:T(8,128)(2,1)} async-done(((bf16[48,2432]{1,0:T(8,128)(2,1)}), bf16[768,2432]{1,0:T(8,128)(2,1)}) %all-gather.5.cloned.1.call-update) | async-done | bytes 3735568 | tf_op jit(solution)/shard_map/all_gather | solution.py:925
  75.4 9.6 %fusion.query_ref.key_ref.value_ref = bf16[1,2048,2304]{2,1,0:T(8,128)(2,1)} fusion(bf16[2048,768]{1,0:T(8,128)(2,1)S(1)} %multiply_convert_fusion.rows_ref, bf16[768,2432]{1,0:T(8,128)(2,1)S(1)} %copy-done.11), kind=kOutput, calls=%fused_computation.1 | convolution fusion | flops 7252475904 | bytes 16121856 | tf_op jit(solution)/shard_map/dot_general | solution.py:38
  85.4 71.5 %attend_forward.3 = (bf16[1,2048,768]{2,1,0:T(8,128)(2,1)}, f32[1,2048,768]{2,1,0:T(8,128)}, f32[1,2048,768]{2,1,0:T(8,128)}) custom-call(s32[2]{0:T(128)} %pad_add_fusion.1.scalars_ref, bf16[1,2048,2304]{2,1,0:T(8,128)(2,1)} %fusion.query_ref.key_ref.value_ref, bf16[1,2048,2304]{2,1,0:T(8,128)(2,1)} %fusion.query_ref.key_ref.value_ref, ...), custom_call_target="tpu_custom_call" | custom-call | flops 1000 | bytes 1000 | tf_op jit(solution)/shard_map/attend_forward/pallas_call | solution.py:734
  156.9 4.7 turn_rows.1.left_ref
  174.0 44.3 %layer_forward.2 = (f32[2048,768]{1,0:T(8,128)}, bf16[768,2048]{1,0:T(8,128)(2,1)}, bf16[2048,4096]{1,0:T(8,128)(2,1)}, bf16[2048,2048]{1,0:T(8,128)(2,1)}, bf16...) custom-call(bf16[2048,768]{1,0:T(8,128)(2,1)} %bitcast.143, ...), custom_call_target="tpu_custom_call" | custom-call | flops 1000 | bytes 1000 | tf_op jit(solution)/shard_map/layer_forward/pallas_call | solution.py:550
  224.5 7.6 fusion.2.query_ref.key_ref.value_ref
  233.5 23.7 %attend_forward.4 = (bf16[1,1024,768]{2,1,0:T(8,128)(2,1)}, f32[1,1024,768]{2,1,0:T(8,128)}, f32[1,1024,768]{2,1,0:T(8,128)}) custom-call(s32[2]{0:T(128)} %pad_add_fusion.scalars_ref, bf16[1,1024,2304]{2,1,0:T(8,128)(2,1)} %fusion.2.query_ref.key_ref.value_ref, bf16[1,1024,2304]{2,1,0:T(8,128)(2,1)} %fusion.2.query_ref.key_ref.value_ref, ...), custom_call_target="tpu_custom_call" | custom-call | flops 1000 | bytes 1000 | tf_op jit(solution)/shard_map/attend_forward/pallas_call | solution.py:734
  263.7 7.0 fusion.1.key_ref.value_ref
  273.3 40.4 %attend_forward.5 = (bf16[1,1024,768]{2,1,0:T(8,128)(2,1)}, f32[1,1024,768]{2,1,0:T(8,128)}, f32[1,1024,768]{2,1,0:T(8,128)}) custom-call(s32[2]{0:T(128)} %pad_add_fusion.1.scalars_ref, bf16[1,1024,768]{2,1,0:T(8,128)(2,1)} %fusion.9.query_ref, bf16[1,2048,1536]{2,1,0:T(8,128)(2,1)} %fusion.1.key_ref.value_ref, bf16[1,2048,1536]{2,1,0:T(8,128)(2,1)} %fusion.1.key_ref.value_ref), custom_call_target="tpu_custom_call" | custom-call | flops 1000 | bytes 1000 | tf_op jit(solution)/shard_map/attend_forward/pallas_call | solution.py:734
  313.8 4.7 all-gather.11.cloned.1.call-done.gate_up_ref.packed_ref.output_ref
  318.4 25.1 %layer_forward.3 = (f32[1024,768]{1,0:T(8,128)}, bf16[768,1024]{1,0:T(8,128)(2,1)}, bf16[1024,4096]{1,0:T(8,128)(2,1)}, bf16[2048,1024]{1,0:T(8,128)(2,1)}, bf16[1024,768]{1,0:T(8,128)(2,1)}) custom-call(bf16[1024,768]{1,0:T(8,128)(2,1)} %bitcast.146, f32[1024,768]{1,0:T(8,128)} %copy-done.2, ...), custom_call_target="tpu_custom_call" | custom-call | flops 1000 | bytes 1000 | tf_op jit(solution)/shard_map/layer_forward/pallas_call | solution.py:550
  343.6 24.0 %layer_backward.2 = (bf16[1024,4096]{1,0:T(8,128)(2,1)}, f32[1024,768]{1,0:T(8,128)}, bf16[1024,768]{1,0:T(8,128)(2,1)}, bf16[1024,768]{1,0:T(8,128)(2,1)}, f32[8,768]{1,0:T(8,128)}) custom-call(bf16[1024,768]{1,0:T(8,128)(2,1)} %bitcast.139, bf16[1024,4096]{1,0:T(8,128)(2,1)} %get-tuple-element.140.slopes_ref, f32[1024,768]{1,0:T(8,128)} %get-tuple-element.141.middle_ref, ...), custom_call_target="tpu_custom_call" | custom-call | flops 1000 | bytes 1000 | tf_op jit(solution)/shard_map/layer_backward/pallas_call | solution.py:550
  367.5 10.9 %weight_grad.9.refs_0_ = bf16[768,6144]{1,0:T(8,128)(2,1)} custom-call(bf16[768,1024]{1,0:T(8,128)(2,1)} %get-tuple-element.139.left_ref, bf16[1024,4096]{1,0:T(8,128)(2,1)} %get-tuple-element.142.right_ref), custom_call_target="tpu_custom_call" | custom-call | flops 1000 | bytes 1000 | tf_op jit(solution)/shard_map/weight_grad/pallas_call | solution.py:665
  378.4 7.2 down_grad.2
  385.8 4.5 weight_grad.10.refs_0_
  390.2 76.1 %attend_backward.3 = (bf16[1,1024,768]{2,1,0:T(8,128)(2,1)}, bf16[1,2048,1536]{2,1,0:T(8,128)(2,1)}) custom-call(s32[2]{0:T(128)} %pad_add_fusion.1.scalars_ref, bf16[1,1024,768]{2,1,0:T(8,128)(2,1)} %fusion.9.query_ref, bf16[1,2048,1536]{2,1,0:T(8,128)(2,1)} %fusion.1.key_ref.value_ref, bf16[1,2048,1536]{2,1,0:T(8,128)(2,1)} %fusion.1.key_ref.value_ref, ...), custom_call_target="tpu_custom_call" | custom-call | flops 1000 | bytes 1000 | tf_op jit(solution)/shard_map/attend_backward/pallas_call | solution.py:796
  466.3 4.5 weight_grad.11.refs_0_
  470.8 9.5 %weight_grad.12 = bf16[768,3072]{1,0:T(8,128)(2,1)} custom-call(bf16[768,2048]{1,0:T(8,128)(2,1)} %get-tuple-element.127.left_ref, bf16[2048,1536]{1,0:T(8,128)(2,1)} %bitcast.137, bf16[768,3072]{1,0:T(8,128)(2,1)} %weight_grad.11.refs_0_), custom_call_target="tpu_custom_call", output_to_operand_aliasing={{}: (2, {})} | custom-call | flops 1000 | bytes 1000 | tf_op jit(solution)/shard_map/weight_grad/pallas_call | solution.py:665
  483.9 9.9 %project_back.4 = (f32[1024,768]{1,0:T(8,128)}, f32[8,768]{1,0:T(8,128)}, bf16[1024,768]{1,0:T(8,128)(2,1)}, bf16[1024,768]{1,0:T(8,128)(2,1)}) custom-call(bf16[1024,768]{1,0:T(8,128)(2,1)} %bitcast.149, bf16[768,3072]{1,0:T(8,128)(2,1)} %all-gather.9.cloned.1.call-done.refs_1_.refs_5_, f32[1024,768]{1,0:T(8,128)} %get-tuple-element.152.refs_2_, ...), custom_call_target="tpu_custom_call" | custom-call | flops 1000 | bytes 1000 | tf_op jit(solution)/shard_map/project_back/pallas_call | solution.py:550
  498.2 36.9 %attend_backward.4 = bf16[1,1024,2304]{2,1,0:T(8,128)(2,1)} custom-call(s32[2]{0:T(128)} %pad_add_fusion.scalars_ref, bf16[1,1024,2304]{2,1,0:T(8,128)(2,1)} %fusion.2.query_ref.key_ref.value_ref, bf16[1,1024,2304]{2,1,0:T(8,128)(2,1)} %fusion.2.query_ref.key_ref.value_ref, bf16[1,1024,2304]{2,1,0:T(8,128)(2,1)} %fusion.2.query_ref.key_ref.value_ref, ...), custom_call_target="tpu_custom_call" | custom-call | flops 1000 | bytes 1000 | tf_op jit(solution)/shard_map/attend_backward/pallas_call | solution.py:796
  535.1 8.1 weight_grad.14
  543.3 13.8 %project_back.6 = (f32[2048,768]{1,0:T(8,128)}, f32[8,768]{1,0:T(8,128)}, bf16[2048,768]{1,0:T(8,128)(2,1)}) custom-call(bf16[2048,1536]{1,0:T(8,128)(2,1)} %bitcast.138, bf16[768,3072]{1,0:T(8,128)(2,1)} %all-gather.9.cloned.1.call-done.refs_1_.refs_5_, bf16[2048,768]{1,0:T(8,128)(2,1)} %bitcast.145, f32[2048,768]{1,0:T(8,128)} %get-tuple-element.167.refs_3_, ...), custom_call_target="tpu_custom_call" | custom-call | flops 1000 | bytes 1000 | tf_op jit(solution)/shard_map/project_back/pallas_call | solution.py:550
  557.1 39.3 %layer_backward.3 = (bf16[2048,4096]{1,0:T(8,128)(2,1)}, f32[2048,768]{1,0:T(8,128)}, bf16[2048,768]{1,0:T(8,128)(2,1)}, bf16[2048,768]{1,0:T(8,128)(2,1)}, f32[8,768]{1,0:T(8,128)}) custom-call(f32[2048,768]{1,0:T(8,128)} %get-tuple-element.168.grad_ref, bf16[2048,4096]{1,0:T(8,128)(2,1)} %get-tuple-element.169.slopes_ref, ...), custom_call_target="tpu_custom_call" | custom-call | flops 1000 | bytes 1000 | tf_op jit(solution)/shard_map/layer_backward/pallas_call | solution.py:550
  596.4 18.3 %weight_grad.15.refs_0_ = bf16[768,6912]{1,0:T(8,128)(2,1)} custom-call(bf16[768,2048]{1,0:T(8,128)(2,1)} %get-tuple-element.174.left_ref, bf16[2048,4096]{1,0:T(8,128)(2,1)} %get-tuple-element.175.right_ref), custom_call_target="tpu_custom_call" | custom-call | flops 1000 | bytes 1000 | tf_op jit(solution)/shard_map/weight_grad/pallas_call | solution.py:665
  614.7 10.8 %down_grad.3.refs_0_ = bf16[768,6912]{1,0:T(8,128)(2,1)} custom-call(bf16[2048,2048]{1,0:T(8,128)(2,1)} %get-tuple-element.172.hidden_ref, bf16[2048,768]{1,0:T(8,128)(2,1)} %get-tuple-element.173.right_ref, bf16[768,6912]{1,0:T(8,128)(2,1)} %weight_grad.15.refs_0_), custom_call_target="tpu_custom_call", output_to_operand_aliasing={{}: (2, {})} | custom-call | flops 1000 | bytes 1000 | tf_op jit(solution)/shard_map/down_grad/pallas_call | solution.py:665
  625.5 6.6 weight_grad.16
  635.1 10.2 %project_back.5 = (f32[1024,768]{1,0:T(8,128)}, f32[8,768]{1,0:T(8,128)}) custom-call(bf16[1024,2304]{1,0:T(8,128)(2,1)} %bitcast.135, bf16[768,9216]{1,0:T(8,128)(2,1)} %all-gather.7.cloned.1.call-done.gate_up_ref.packed_ref.output_ref.refs_1_, f32[1024,768]{1,0:T(8,128)} %get-tuple-element.161.refs_2_, bf16[1024,768]{1,0:T(8,128)(2,1)} %bitcast.136, ...), custom_call_target="tpu_custom_call" | custom-call | flops 1000 | bytes 1000 | tf_op jit(solution)/shard_map/project_back/pallas_call | solution.py:550
  647.6 141.2 %attend_backward.5 = bf16[1,2048,2304]{2,1,0:T(8,128)(2,1)} custom-call(s32[2]{0:T(128)} %pad_add_fusion.1.scalars_ref, bf16[1,2048,2304]{2,1,0:T(8,128)(2,1)} %fusion.query_ref.key_ref.value_ref, bf16[1,2048,2304]{2,1,0:T(8,128)(2,1)} %fusion.query_ref.key_ref.value_ref, bf16[1,2048,2304]{2,1,0:T(8,128)(2,1)} %fusion.query_ref.key_ref.value_ref, ...), custom_call_target="tpu_custom_call" | custom-call | flops 1000 | bytes 1000 | tf_op jit(solution)/shard_map/attend_backward/pallas_call | solution.py:796
  791.1 12.1 %weight_grad.17 = bf16[768,2304]{1,0:T(8,128)(2,1)} custom-call(bf16[768,2048]{1,0:T(8,128)(2,1)} %turn_rows.1.left_ref, bf16[2048,2304]{1,0:T(8,128)(2,1)} %bitcast.130), custom_call_target="tpu_custom_call" | custom-call | flops 1000 | bytes 1000 | tf_op jit(solution)/shard_map/weight_grad/pallas_call | solution.py:665
  809.3 16.8 %project_back.7 = (f32[2048,768]{1,0:T(8,128)}, f32[8,768]{1,0:T(8,128)}) custom-call(bf16[2048,2304]{1,0:T(8,128)(2,1)} %bitcast.131, bf16[768,2432]{1,0:T(8,128)(2,1)} %all-gather.5.cloned.1.call-done.refs_1_, f32[2048,768]{1,0:T(8,128)} %get-tuple-element.195.refs_2_, f32[2048,768]{1,0:T(8,128)} %copy-done, f32[8,768]{1,0:T(8,128)} %copy-done.18), custom_call_target="tpu_custom_call" | custom-call | flops 1000 | bytes 1000 | tf_op jit(solution)/shard_map/project_back/pallas_call | solution.py:550
  861.6 14.6 %collective-permute-done.18 = bf16[48,8]{0,1:T(8,128)(2,1)S(1)} collective-permute-done((bf16[48,8]{0,1:T(8,128)(2,1)S(1)}, bf16[48,8]{0,1:T(8,128)(2,1)S(1)}, u32[]{:S(2)}, u32[]{:S(2)}) %collective-permute-start.18) | collective-permute-done | bytes 800 | tf_op jit(solution)/shard_map/ppermute | solution.py:893
  878.0 6.3 place_halves.1
  (306 shorter events, 121.9 us)
Async XLA Ops:
  7.2 54.8 %all-gather.5.cloned.1.call-start = ((), (), s32[]{:S(2)}) async-start(), calls=%async_computation.5 | async-start | bytes 3969024 | tf_op jit(solution)/shard_map/all_gather | solution.py:925
  11.3 162.7 %all-gather.7.cloned.1.call-start = ((), (), s32[]{:S(2)}) async-start(), calls=%async_computation.6 | async-start | bytes 15040512 | tf_op jit(solution)/shard_map/all_gather | solution.py:925
  14.9 242.3 %all-gather.9.cloned.1.call-start = ((), (), s32[]{:S(2)}) async-start(), calls=%async_computation.7 | async-start | bytes 5013504 | tf_op jit(solution)/shard_map/all_gather | solution.py:925
  16.2 302.2 %all-gather.11.cloned.1.call-start = ((), (), s32[]{:S(2)}) async-start(), calls=%async_computation.8 | async-start | bytes 11280384 | tf_op jit(solution)/shard_map/all_gather | solution.py:925
  19.5 43.6 %collective-permute-start = (bf16[1024,768]{1,0:T(8,128)(2,1)}, bf16[1024,768]{1,0:T(8,128)(2,1)S(1)}, u32[]{:S(2)}, u32[]{:S(2)}) collective-permute-start(bf16[1024,768]{1,0:T(8,128)(2,1)} %get-tuple-element.229), channel_id=1, source_target_pairs={{0,1},{1,0},{2,3},{3,2},{4,5},{5,4},{6,7},{7,6},{8,9},{9,8},{10,11... | collective-permute-start | bytes 4718600 | tf_op jit(solution)/shard_map/ppermute | solution.py:893
  66.8 99.1 %collective-permute-start.2 = (bf16[1024,768]{1,0:T(8,128)(2,1)}, bf16[1024,768]{1,0:T(8,128)(2,1)}, u32[]{:S(2)}, u32[]{:S(2)}) collective-permute-start(bf16[1024,768]{1,0:T(8,128)(2,1)} %get-tuple-element.227), channel_id=1, source_target_pairs={{0,1},{1,0},{2,3},{3,2},{4,5},{5,4},{6,7},{7,6},{8,9},{9,8},{10,11... | collective-permute-start | bytes 4718600 | tf_op jit(solution)/shard_map/ppermute | solution.py:893
  69.6 92.0 %collective-permute-start.1 = (bf16[512,768]{1,0:T(8,128)(2,1)}, bf16[512,768]{1,0:T(8,128)(2,1)}, u32[]{:S(2)}, u32[]{:S(2)}) collective-permute-start(bf16[512,768]{1,0:T(8,128)(2,1)} %get-tuple-element.235), channel_id=1, source_target_pairs={{0,1},{1,0},{2,3},{3,2},{4,5},{5,4},{6,7},{7,6},{8,9},{9,8},{10,11... | collective-permute-start | bytes 2359304 | tf_op jit(solution)/shard_map/ppermute | solution.py:893
  71.4 90.1 %collective-permute-start.3 = (bf16[512,768]{1,0:T(8,128)(2,1)}, bf16[512,768]{1,0:T(8,128)(2,1)}, u32[]{:S(2)}, u32[]{:S(2)}) collective-permute-start(bf16[512,768]{1,0:T(8,128)(2,1)} %get-tuple-element.233), channel_id=1, source_target_pairs={{0,1},{1,0},{2,3},{3,2},{4,5},{5,4},{6,7},{7,6},{8,9},{9,8},{10,11... | collective-permute-start | bytes 2359304 | tf_op jit(solution)/shard_map/ppermute | solution.py:893
  166.0 91.3 %copy-start.3 = (bf16[1,1024,768]{2,1,0:T(8,128)(2,1)}, bf16[1,1024,768]{2,1,0:T(8,128)(2,1)S(1)}, u32[]{:S(2)}) copy-start(bf16[1,1024,768]{2,1,0:T(8,128)(2,1)S(1)} %get-tuple-element.125) | copy-start | bytes 4718596
  174.0 44.6 %copy-start.39 = (bf16[48,768]{1,0:T(8,128)(2,1)S(1)}, bf16[48,768]{1,0:T(8,128)(2,1)}, u32[]{:S(2)}) copy-start(bf16[48,768]{1,0:T(8,128)(2,1)} %param.35) | copy-start | bytes 221188
  219.5 323.8 %reduce-scatter.6.cloned.1.call-start = ((), (), s32[]{:S(2)}) async-start(), calls=%async_computation.9 | async-start | bytes 10027008 | tf_op jit(solution)/shard_map/reduce_scatter | solution.py:928
  232.1 81.6 %collective-permute-start.4 = (bf16[1024,768]{1,0:T(8,128)(2,1)}, bf16[1024,768]{1,0:T(8,128)(2,1)S(1)}, u32[]{:S(2)}, u32[]{:S(2)}) collective-permute-start(bf16[1024,768]{1,0:T(8,128)(2,1)} %get-tuple-element.224), channel_id=1, source_target_pairs={{0,1},{1,0},{2,3},{3,2},{4,5},{5,4},{6,7},{7,6},{8,9},{9,8},{10,11... | collective-permute-start | bytes 4718600 | tf_op jit(solution)/shard_map/ppermute | solution.py:893
  385.7 246.4 %reduce-scatter.10.cloned.1.call-start = ((), (), s32[]{:S(2)}) async-start(), calls=%async_computation.11 | async-start | bytes 5013504 | tf_op jit(solution)/shard_map/reduce_scatter | solution.py:928
  480.4 310.7 %reduce-scatter.8.cloned.1.call-start = ((), (), s32[]{:S(2)}) async-start(), calls=%async_computation.10 | async-start | bytes 5013504 | tf_op jit(solution)/shard_map/reduce_scatter | solution.py:928
  482.8 60.4 %collective-permute-start.5 = (bf16[512,768]{1,0:T(8,128)(2,1)S(1)}, bf16[512,768]{1,0:T(8,128)(2,1)S(1)}, u32[]{:S(2)}, u32[]{:S(2)}) collective-permute-start(bf16[512,768]{1,0:T(8,128)(2,1)S(1)} %get-tuple-element.230), channel_id=1, source_target_pairs={{0,1},{1,0},{2,3},{3,2},{4,5},{5,4},{6,7},{7,6},{8,9},{9,8},{10,11... | collective-permute-start | bytes 2359304 | tf_op jit(solution)/shard_map/ppermute | solution.py:893
  543.3 247.8 %reduce-scatter.12.cloned.1.call-start = ((), (), s32[]{:S(2)}) async-start(), calls=%async_computation.12 | async-start | bytes 11280384 | tf_op jit(solution)/shard_map/reduce_scatter | solution.py:928
  632.1 244.0 %reduce-scatter.14.cloned.1.call-start = ((), (), s32[]{:S(2)}) async-start(), calls=%async_computation.13 | async-start | bytes 3760128 | tf_op jit(solution)/shard_map/reduce_scatter | solution.py:928
  633.0 155.9 %collective-permute-start.8 = (bf16[48,3072]{1,0:T(8,128)(2,1)S(1)}, bf16[48,3072]{1,0:T(8,128)(2,1)S(1)}, u32[]{:S(2)}, u32[]{:S(2)}) collective-permute-start(bf16[48,3072]{1,0:T(8,128)(2,1)S(1)} %copy-done.32), channel_id=1, source_target_pairs={{0,1},{1,0},{2,3},{3,2},{4,5},{5,4},{6,7},{7,6},{8,9},{9,8},{10,11... | collective-permute-start | bytes 884744 | tf_op jit(solution)/shard_map/ppermute | solution.py:893
  634.0 155.9 %collective-permute-start.7 = (bf16[48,6144]{1,0:T(8,128)(2,1)S(1)}, bf16[48,6144]{1,0:T(8,128)(2,1)}, u32[]{:S(2)}, u32[]{:S(2)}) collective-permute-start(bf16[48,6144]{1,0:T(8,128)(2,1)S(1)} %copy-done.29), channel_id=1, source_target_pairs={{0,1},{1,0},{2,3},{3,2},{4,5},{5,4},{6,7},{7,6},{8,9},{9,8},{10,11... | collective-permute-start | bytes 1769480 | tf_op jit(solution)/shard_map/ppermute | solution.py:893
  646.8 144.3 %collective-permute-start.6 = (bf16[512,768]{1,0:T(8,128)(2,1)S(1)}, bf16[512,768]{1,0:T(8,128)(2,1)}, u32[]{:S(2)}, u32[]{:S(2)}) collective-permute-start(bf16[512,768]{1,0:T(8,128)(2,1)S(1)} %dynamic-slice_convert_fusion.1), channel_id=1, source_target_pairs={{0,1},{1,0},{2,3},{3,2},{4,5},{5,4},{6,7},{7,6},{8,9},{9,8},{10,11... | collective-permute-start | bytes 2359304 | tf_op jit(solution)/shard_map/ppermute | solution.py:893
  647.6 141.2 %copy-start.19 = (f32[1024,768]{1,0:T(8,128)S(1)}, f32[1024,768]{1,0:T(8,128)}, u32[]{:S(2)}) copy-start(f32[1024,768]{1,0:T(8,128)} %get-tuple-element.162) | copy-start | bytes 9437188
  803.2 30.6 %collective-permute-start.10 = (bf16[48,6912]{1,0:T(8,128)(2,1)}, bf16[48,6912]{1,0:T(8,128)(2,1)}, u32[]{:S(2)}, u32[]{:S(2)}) collective-permute-start(bf16[48,6912]{1,0:T(8,128)(2,1)} %reduce-scatter.12.cloned.1.call-done), channel_id=1, source_target_pairs={{0,1},{1,0},{2,3},{3,2},{4,5},{5,4},{6,7},{7,6},{8,9},{9,8},{10,11... | collective-permute-start | bytes 1990664 | tf_op jit(solution)/shard_map/ppermute | solution.py:893
  808.6 25.3 %collective-permute-start.9 = (bf16[48,3072]{1,0:T(8,128)(2,1)}, bf16[48,3072]{1,0:T(8,128)(2,1)}, u32[]{:S(2)}, u32[]{:S(2)}) collective-permute-start(bf16[48,3072]{1,0:T(8,128)(2,1)} %reduce-scatter.8.cloned.1.call-done), channel_id=1, source_target_pairs={{0,1},{1,0},{2,3},{3,2},{4,5},{5,4},{6,7},{7,6},{8,9},{9,8},{10,11... | collective-permute-start | bytes 884744 | tf_op jit(solution)/shard_map/ppermute | solution.py:893
  835.9 12.7 %collective-permute-start.12 = (f32[8,768]{1,0:T(8,128)S(1)}, f32[8,768]{1,0:T(8,128)S(1)}, u32[]{:S(2)}, u32[]{:S(2)}) collective-permute-start(f32[8,768]{1,0:T(8,128)S(1)} %concatenate.31), channel_id=1, source_target_pairs={{0,2},{2,0},{4,6},{6,4},{8,10},{10,8},{12,14},{14,12},{16,18},{18,... | collective-permute-start | bytes 73736 | tf_op jit(solution)/shard_map/ppermute | solution.py:935
  836.0 12.6 %collective-permute-start.13 = (f32[8,768]{1,0:T(8,128)S(1)}, f32[8,768]{1,0:T(8,128)S(1)}, u32[]{:S(2)}, u32[]{:S(2)}) collective-permute-start(f32[8,768]{1,0:T(8,128)S(1)} %concatenate.31), channel_id=1, source_target_pairs={{0,4},{2,6},{4,0},{6,2},{8,12},{10,14},{12,8},{14,10},{16,20},{18,... | collective-permute-start | bytes 73736 | tf_op jit(solution)/shard_map/ppermute | solution.py:935
  836.2 12.4 %collective-permute-start.14 = (f32[8,768]{1,0:T(8,128)S(1)}, f32[8,768]{1,0:T(8,128)S(1)}, u32[]{:S(2)}, u32[]{:S(2)}) collective-permute-start(f32[8,768]{1,0:T(8,128)S(1)} %concatenate.31), channel_id=1, source_target_pairs={{0,6},{2,4},{4,2},{6,0},{8,14},{10,12},{12,10},{14,8},{16,22},{18,... | collective-permute-start | bytes 73736 | tf_op jit(solution)/shard_map/ppermute | solution.py:935
  839.1 38.9 %collective-permute-start.11 = (bf16[1024,768]{1,0:T(8,128)(2,1)}, bf16[1024,768]{1,0:T(8,128)(2,1)}, u32[]{:S(2)}, u32[]{:S(2)}) collective-permute-start(bf16[1024,768]{1,0:T(8,128)(2,1)} %dynamic-slice_convert_fusion), channel_id=1, source_target_pairs={{0,1},{1,0},{2,3},{3,2},{4,5},{5,4},{6,7},{7,6},{8,9},{9,8},{10,11... | collective-permute-start | bytes 4718600 | tf_op jit(solution)/shard_map/ppermute | solution.py:893
  848.6 7.2 collective-permute-start.15
  848.9 6.9 collective-permute-start.16
  850.8 5.6 collective-permute-start.17
  856.5 19.6 %collective-permute-start.18 = (bf16[48,8]{0,1:T(8,128)(2,1)S(1)}, bf16[48,8]{0,1:T(8,128)(2,1)S(1)}, u32[]{:S(2)}, u32[]{:S(2)}) collective-permute-start(bf16[48,8]{0,1:T(8,128)(2,1)S(1)} %fusion.17), channel_id=1, source_target_pairs={{0,1},{1,0},{2,3},{3,2},{4,5},{5,4},{6,7},{7,6},{8,9},{9,8},{10,11... | collective-permute-start | bytes 2312 | tf_op jit(solution)/shard_map/ppermute | solution.py:893
  876.1 8.1 collective-permute-start.19
  (57 other events, 422.3 us)
Sparse Core Ops, SparseCore 0:
  11.4 50.5 all-gather.4
  64.3 109.6 all-gather.6
  176.8 51.4 all-gather.8
  231.0 87.3 all-gather.10
  385.8 109.6 reduce-scatter.5
  499.7 75.2 reduce-scatter.9
  578.9 74.5 reduce-scatter.7
  658.1 119.3 reduce-scatter.11
  803.3 67.9 reduce-scatter.13
